TPU v7x, 128 devices: a whole 4x4x4 slice. The times are simulated.
128 devices in a mesh: field: 4 (over x), gz: 32 (over y, z, core).
Axes of the slice: x: 4, y: 4, z: 4, core: 2. Of those that a mesh axis runs over, the one named last changes fastest.
Arguments:
- fields: bfloat16 [2048, 2, 8, 16, 256], P('gz', None, 'field'), may hold values from -8 to 8
- shells: int32 [2048, 16, 256], P('gz'), may hold values from 0 to 255
- mubins: int32 [2048, 16, 256], P('gz'), may hold values from 0 to 7, as said below
Outputs:
- power: float32 [3, 8, 256], replicated
Inputs may be any that keep to these rules, and one draw needn't show every extreme that they name: `mubins`: A cell's mu-bin index is never above its k-shell index.
All inputs are finite; a program needn't handle non-finite values.
Results may differ from a plain program's by a relative error of at most 0.00052.
Values may be sent and summed in bfloat16 or wider, within the bound.
No kernel may reach another device: no remote copies, remote signals or barrier semaphores. Data moves between devices by JAX's collectives and lax.ppermute only.
A program may use at most 128 MiB of HBM per device.

v0:
```python
import math

import jax
import jax.numpy as jnp
import numpy as np
from jax import lax
from jax.sharding import PartitionSpec as P

NZ = 2048
SHELLS = 256
MUBINS = 8


def broadcast(value, axis, source):
    kept = jnp.where(lax.axis_index(axis) == source, value, 0).astype(value.dtype)
    return lax.psum(kept, axis)


def make_coef():
    table = np.zeros((3, 8, 7), np.float32)
    table[0, 0, 0] = 1.0
    table[1, 1, 0] = 1.0
    table[2, 1, 0] = -0.5
    table[2, 2, 1] = 1.5
    table[2, 3, 2] = 1.5
    table[2, 4, 3] = 1.5
    table[2, 5, 4] = 3.0
    table[2, 6, 5] = 3.0
    table[2, 7, 6] = 3.0
    return table


def dft_tables(length):
    index = jnp.arange(length, dtype=jnp.int32)
    product = index[:, None] * index[None, :] % length
    angle = product.astype(jnp.float32) * (2.0 * math.pi / length)
    factor = 1.0 / math.sqrt(length)
    return (
        (jnp.cos(angle) * factor).astype(jnp.bfloat16),
        (jnp.sin(angle) * factor).astype(jnp.bfloat16),
    )


def transform(lines, cos_table, sin_table):
    length, _, items, columns = lines.shape
    flat = lines.reshape(length, 2 * items * columns)
    first = jnp.dot(cos_table, flat, preferred_element_type=jnp.float32).reshape(
        length, 2, items, columns
    )
    second = jnp.dot(sin_table, flat, preferred_element_type=jnp.float32).reshape(
        length, 2, items, columns
    )
    real_part = first[:, 0] + second[:, 1]
    imag_part = first[:, 1] - second[:, 0]
    return jnp.stack([real_part, imag_part], axis=1)


def monomials(wave_x, wave_y, wave_z):
    square = wave_x * wave_x + wave_y * wave_y + wave_z * wave_z
    ones = jnp.ones_like(square)
    return jnp.stack(
        [
            ones,
            wave_x * wave_x / square,
            wave_y * wave_y / square,
            wave_z * wave_z / square,
            wave_x * wave_y / square,
            wave_x * wave_z / square,
            wave_y * wave_z / square,
        ]
    )


def bin_cells(values, shell_ids, mu_ids):
    cells = values.shape[1]
    block = math.gcd(cells, 32768)
    blocks = cells // block
    value_blocks = values.reshape(3, blocks, block).transpose(1, 0, 2)
    shell_blocks = shell_ids.reshape(blocks, block)
    mu_blocks = mu_ids.reshape(blocks, block)

    def step(total, pieces):
        value_piece, shell_piece, mu_piece = pieces
        mu_hot = (mu_piece[None, :] == jnp.arange(MUBINS, dtype=jnp.int32)[:, None]).astype(
            jnp.bfloat16
        )
        rows = (value_piece[:, None, :] * mu_hot[None]).reshape(3 * MUBINS, block)
        rows = jnp.concatenate([rows, mu_hot], axis=0)
        shell_hot = (shell_piece[None, :] == jnp.arange(SHELLS, dtype=jnp.int32)[:, None]).astype(
            jnp.bfloat16
        )
        return (
            total
            + lax.dot_general(
                rows, shell_hot, (((1,), (1,)), ((), ())), preferred_element_type=jnp.float32
            ),
            None,
        )

    start = jnp.zeros((4 * MUBINS, SHELLS), jnp.float32)
    total, _ = lax.scan(step, start, (value_blocks, shell_blocks, mu_blocks))
    return total


def body(fields, shells, mubins):
    depth_local, _, local_fields, planes, yrows = fields.shape
    plane_rows = planes * yrows
    own = fields.reshape(depth_local, 2, local_fields, plane_rows)
    cos_table, sin_table = dft_tables(NZ)
    spectra_lines = transform(
        lax.all_to_all(own, "gz", split_axis=3, concat_axis=0, tiled=True), cos_table, sin_table
    )
    spectra = lax.all_to_all(spectra_lines, "gz", split_axis=0, concat_axis=3, tiled=True)
    twenty_spec = broadcast(spectra[:, :, 0], "field", 0)
    shell_map = shells.reshape(depth_local, plane_rows)
    mu_map = mubins.reshape(depth_local, plane_rows)
    depth_first = lax.axis_index("gz") * depth_local
    depth_span, column_span = shell_map.shape
    depth_index = depth_first + jnp.arange(depth_span, dtype=jnp.int32)
    wave_z = jnp.where(depth_index >= NZ // 2, depth_index - NZ, depth_index).astype(jnp.float32)
    column_index = jnp.arange(column_span, dtype=jnp.int32)
    wave_x = (NZ // 4 + column_index // yrows).astype(jnp.float32)
    wave_y = (NZ // 8 + column_index % yrows).astype(jnp.float32)
    terms = monomials(
        wave_x[None, :] + jnp.zeros((depth_span, column_span), jnp.float32),
        wave_y[None, :],
        wave_z[:, None],
    )
    coef_rows = lax.dynamic_slice_in_dim(
        jnp.asarray(make_coef()), lax.axis_index("field") * local_fields, local_fields, 1
    )
    weights = jnp.einsum("mlj,jzc->mlzc", coef_rows, terms, precision=lax.Precision.HIGHEST)
    cross = twenty_spec[:, 0][:, None] * spectra[:, 0] + twenty_spec[:, 1][:, None] * spectra[:, 1]
    contrib = jnp.sum(weights * jnp.transpose(cross, (1, 0, 2))[None], axis=1).astype(jnp.bfloat16)
    partial_bins = bin_cells(
        contrib.reshape(3, depth_span * column_span), shell_map.reshape(-1), mu_map.reshape(-1)
    )
    count_gate = (lax.axis_index("field") == 0).astype(jnp.float32)
    partial_bins = jnp.concatenate(
        [partial_bins[: 3 * MUBINS], partial_bins[3 * MUBINS :] * count_gate], axis=0
    )
    total = lax.psum(partial_bins, ("field", "gz"))
    sums = total[: 3 * MUBINS].reshape(3, MUBINS, SHELLS)
    counts = total[3 * MUBINS :]
    return sums / jnp.maximum(counts, 1.0)[None]


def solution(mesh):
    in_specs = (P("gz", None, "field", None, None), P("gz", None, None), P("gz", None, None))
    out_specs = P()
    return jax.shard_map(body, mesh=mesh, in_specs=in_specs, out_specs=out_specs, check_vma=False)
```

profile of v0, /device:TPU:0, one launch (start us, length us, event | category | flops | bytes accessed | tf_op | source)
XLA Modules:
  0.0 527.3 jit_solution(12620852004919431536)
XLA Ops:
  6.5 8.0 %copy.24 = bf16[64,2,2,16,256]{0,2,1,4,3:T(2,128)(2,1)} copy(bf16[64,2,2,16,256]{4,3,2,1,0:T(8,128)(2,1)} %param.6) | data formatting | bytes 4194304 | tf_op args[0]
  14.5 9.8 %reshape.520 = bf16[32,2,16384]{2,1,0:T(2,128)(2,1)} reshape(bf16[4096,2,2,64]{3,2,1,0:T(2,128)(2,1)} %bitcast.84) | data formatting | bytes 4194304
  24.3 8.4 %all-to-all-start = ((bf16[32,2,16384]{2,1,0:T(2,128)(2,1)}), bf16[32,2,16384]{2,1,0:T(2,128)(2,1)S(1)}, u32[]{:S(2)}, u32[]{:S(2)}) async-start(bf16[32,2,16384]{2,1,0:T(2,128)(2,1)} %reshape.520), calls=%async_computation | async-start | bytes 4194304 | tf_op jit(solution)/shard_map/all_to_all | solution.py:111
  32.9 28.8 %all-to-all-done = bf16[32,2,16384]{2,1,0:T(2,128)(2,1)S(1)} async-done(((bf16[32,2,16384]{2,1,0:T(2,128)(2,1)}), bf16[32,2,16384]{2,1,0:T(2,128)(2,1)S(1)}, u32[]{:S(2)}, u32[]{:S(2)}) %all-to-all-start) | async-done | bytes 2097184 | tf_op jit(solution)/shard_map/all_to_all | solution.py:111
  61.7 4.0 reshape.521
  65.7 6.3 %copy.35 = bf16[64,2,2,32,128]{4,3,0,2,1:T(8,128)(2,1)S(1)} copy(bf16[64,2,2,32,128]{0,2,1,4,3:T(2,128)(2,1)} %bitcast.83) | data formatting | bytes 4194304 | tf_op jit(solution)/shard_map/all_to_all | solution.py:111
  72.0 3.5 copy.26
  75.5 2.7 reshape.514
  78.2 2.5 copy.27
  80.7 66.2 %fusion.20 = f32[2048,2,2,128]{3,0,2,1:T(8,128)S(1)} fusion(bf16[2,2,128,2048]{3,2,1,0:T(8,128)(2,1)} %bitcast.90), kind=kOutput, calls=%fused_computation.28 | convolution fusion | flops 4362076160 | bytes 6291456 | tf_op jit(solution)/shard_map/dot_general | solution.py:50
  147.0 63.9 %fusion.17 = f32[2048,2,2,128]{3,0,2,1:T(8,128)S(1)} fusion(bf16[2,2,128,2048]{3,2,1,0:T(8,128)(2,1)S(1)} %bitcast.91), kind=kOutput, calls=%fused_computation.26 | convolution fusion | flops 4362076160 | bytes 6291456 | tf_op jit(solution)/shard_map/dot_general | solution.py:47
  211.6 12.2 %copy.28 = f32[2048,2,2,128]{3,2,1,0:T(2,128)} copy(f32[2048,2,2,128]{3,0,2,1:T(8,128)S(1)} %pad_maximum_fusion) | data formatting | bytes 8388608 | tf_op jit(solution)/shard_map/stack | solution.py:55
  223.8 4.9 all-to-all-start.1
  234.6 46.7 %all-to-all-done.1 = f32[2048,2,2,128]{3,2,1,0:T(2,128)} async-done(((f32[2048,2,2,128]{3,2,1,0:T(2,128)}), f32[2048,2,2,128]{3,2,1,0:T(2,128)}, u32[]{:S(2)}, u32[]{:S(2)}) %all-to-all-start.1) | async-done | bytes 4194336 | tf_op jit(solution)/shard_map/all_to_all | solution.py:113
  281.3 6.7 %copy.29 = f32[64,2,2,32,128]{4,3,0,2,1:T(8,128)} copy(f32[64,2,2,32,128]{4,2,1,0,3:T(2,128)} %bitcast.13) | data formatting | bytes 8388608 | tf_op jit(solution)/shard_map/all_to_all | solution.py:113
  288.0 4.9 all_to_all.30
  292.9 3.3 fusion.35
  301.0 54.6 %all-reduce.2.cloned.1.call-done = f32[64,2,4096]{2,0,1:T(8,128)} async-done(((f32[64,2,4096]{2,0,1:T(8,128)}), f32[64,2,4096]{2,0,1:T(8,128)}) %all-reduce.2.cloned.1.call-update) | async-done | bytes 2097168 | tf_op jit(solution)/shard_map/psum | solution.py:16
  355.6 1.9 slice_bitcast_fusion.3
  358.9 21.6 %multiply_reduce_fusion = bf16[3,64,4096]{2,0,1:T(4,128)(2,1)S(1)} fusion(f32[7,64,4096]{2,1,0:T(8,128)} %fusion.41, f32[2,64,4096]{2,1,0:T(8,128)S(1)} %fusion.33, f32[3,8,7]{2,0,1:T(4,128)} %constant.91.clone, s32[]{:T(128)S(6)} %select_n.68), kind=kOutput, calls=%fused_computation.32 | convolution fusion | flops 134479872 | bytes 11014148 | tf_op jit(solution)/shard_map/mlj,jzc->mlzc/dot_general | solution.py:132
  382.4 2.7 copy.31
  385.1 69.5 %while.11 = (s32[]{:T(128)}, f32[32,256]{1,0:T(8,128)S(1)}, bf16[8,3,32768]{2,1,0:T(4,128)(2,1)}, s32[8,32768]{1,0:T(8,128)}, s32[8,32768]{1,0:T(8,128)}, /*index=5*/s32[]{:T(128)}, s32[]{:T(128)}) while((s32[]{:T(128)}, f32[32,256]{1,0:T(8,128)S(1)}, bf16[8,3,32768]{2,1,0:T(4,128)(2,1)}, s32[8,32768]{1,0:T(8,128)}, ...), condition=%wide.region_3.4_spmd.clone, body=%wide.region_2.3_spmd.clone.sunk | while | flops 550780928 | bytes 6160487 | solution.py:101
  388.3 5.5 %fusion.86 = f32[32,256]{1,0:T(8,128)S(1)} fusion(s32[32768]{0:T(1024)S(1)} %bitcast.89, bf16[8,32768]{1,0:T(8,128)(2,1)S(1)} %fusion.85, bf16[24,32768]{1,0:T(8,128)(2,1)S(1)} %multiply_bitcast_fusion.2, f32[32,256]{1,0:T(8,128)S(1)} %get-tuple-element.130, pred[]{:T(512)S(6)} %compare.9), kind=kOutput, calls=%fused_computation.7.clone.1 | convolution fusion | flops 549470208 | bytes 2293761 | tf_op jit(solution)/shard_map/while/body/eval_jaxpr/dot_general | solution.py:94
  394.9 1.7 constant_dynamic-slice_fusion.3
  397.0 5.5 %fusion.86 = f32[32,256]{1,0:T(8,128)S(1)} fusion(s32[32768]{0:T(1024)S(1)} %bitcast.89, bf16[8,32768]{1,0:T(8,128)(2,1)S(1)} %fusion.85, bf16[24,32768]{1,0:T(8,128)(2,1)S(1)} %multiply_bitcast_fusion.2, f32[32,256]{1,0:T(8,128)S(1)} %get-tuple-element.130, pred[]{:T(512)S(6)} %compare.9), kind=kOutput, calls=%fused_computation.7.clone.1 | convolution fusion | flops 549470208 | bytes 2293761 | tf_op jit(solution)/shard_map/while/body/eval_jaxpr/dot_general | solution.py:94
  405.7 5.5 %fusion.86 = f32[32,256]{1,0:T(8,128)S(1)} fusion(s32[32768]{0:T(1024)S(1)} %bitcast.89, bf16[8,32768]{1,0:T(8,128)(2,1)S(1)} %fusion.85, bf16[24,32768]{1,0:T(8,128)(2,1)S(1)} %multiply_bitcast_fusion.2, f32[32,256]{1,0:T(8,128)S(1)} %get-tuple-element.130, pred[]{:T(512)S(6)} %compare.9), kind=kOutput, calls=%fused_computation.7.clone.1 | convolution fusion | flops 549470208 | bytes 2293761 | tf_op jit(solution)/shard_map/while/body/eval_jaxpr/dot_general | solution.py:94
  414.4 5.5 %fusion.86 = f32[32,256]{1,0:T(8,128)S(1)} fusion(s32[32768]{0:T(1024)S(1)} %bitcast.89, bf16[8,32768]{1,0:T(8,128)(2,1)S(1)} %fusion.85, bf16[24,32768]{1,0:T(8,128)(2,1)S(1)} %multiply_bitcast_fusion.2, f32[32,256]{1,0:T(8,128)S(1)} %get-tuple-element.130, pred[]{:T(512)S(6)} %compare.9), kind=kOutput, calls=%fused_computation.7.clone.1 | convolution fusion | flops 549470208 | bytes 2293761 | tf_op jit(solution)/shard_map/while/body/eval_jaxpr/dot_general | solution.py:94
  423.1 5.5 %fusion.86 = f32[32,256]{1,0:T(8,128)S(1)} fusion(s32[32768]{0:T(1024)S(1)} %bitcast.89, bf16[8,32768]{1,0:T(8,128)(2,1)S(1)} %fusion.85, bf16[24,32768]{1,0:T(8,128)(2,1)S(1)} %multiply_bitcast_fusion.2, f32[32,256]{1,0:T(8,128)S(1)} %get-tuple-element.130, pred[]{:T(512)S(6)} %compare.9), kind=kOutput, calls=%fused_computation.7.clone.1 | convolution fusion | flops 549470208 | bytes 2293761 | tf_op jit(solution)/shard_map/while/body/eval_jaxpr/dot_general | solution.py:94
  431.8 5.5 %fusion.86 = f32[32,256]{1,0:T(8,128)S(1)} fusion(s32[32768]{0:T(1024)S(1)} %bitcast.89, bf16[8,32768]{1,0:T(8,128)(2,1)S(1)} %fusion.85, bf16[24,32768]{1,0:T(8,128)(2,1)S(1)} %multiply_bitcast_fusion.2, f32[32,256]{1,0:T(8,128)S(1)} %get-tuple-element.130, pred[]{:T(512)S(6)} %compare.9), kind=kOutput, calls=%fused_computation.7.clone.1 | convolution fusion | flops 549470208 | bytes 2293761 | tf_op jit(solution)/shard_map/while/body/eval_jaxpr/dot_general | solution.py:94
  440.5 5.5 %fusion.86 = f32[32,256]{1,0:T(8,128)S(1)} fusion(s32[32768]{0:T(1024)S(1)} %bitcast.89, bf16[8,32768]{1,0:T(8,128)(2,1)S(1)} %fusion.85, bf16[24,32768]{1,0:T(8,128)(2,1)S(1)} %multiply_bitcast_fusion.2, f32[32,256]{1,0:T(8,128)S(1)} %get-tuple-element.130, pred[]{:T(512)S(6)} %compare.9), kind=kOutput, calls=%fused_computation.7.clone.1 | convolution fusion | flops 549470208 | bytes 2293761 | tf_op jit(solution)/shard_map/while/body/eval_jaxpr/dot_general | solution.py:94
  449.2 5.5 %fusion.86 = f32[32,256]{1,0:T(8,128)S(1)} fusion(s32[32768]{0:T(1024)S(1)} %bitcast.89, bf16[8,32768]{1,0:T(8,128)(2,1)S(1)} %fusion.85, bf16[24,32768]{1,0:T(8,128)(2,1)S(1)} %multiply_bitcast_fusion.2, f32[32,256]{1,0:T(8,128)S(1)} %get-tuple-element.130, pred[]{:T(512)S(6)} %compare.9), kind=kOutput, calls=%fused_computation.7.clone.1 | convolution fusion | flops 549470208 | bytes 2293761 | tf_op jit(solution)/shard_map/while/body/eval_jaxpr/dot_general | solution.py:94
  454.7 64.9 %psum.15 = f32[32,256]{1,0:T(8,128)S(1)} all-reduce(f32[32,256]{1,0:T(8,128)S(1)} %pad_maximum_fusion.1), channel_id=1, replica_groups=mesh['field'=4,'gz'=32] {'field','gz'}, use_global_device_ids=true, to_apply=%region_4.5 | all-reduce | flops 8192 | bytes 65536 | tf_op jit(solution)/shard_map/psum | solution.py:142
  (69 shorter events, 38.8 us)
Async XLA Ops:
  24.3 37.4 %all-to-all-start = ((bf16[32,2,16384]{2,1,0:T(2,128)(2,1)}), bf16[32,2,16384]{2,1,0:T(2,128)(2,1)S(1)}, u32[]{:S(2)}, u32[]{:S(2)}) async-start(bf16[32,2,16384]{2,1,0:T(2,128)(2,1)} %reshape.520), calls=%async_computation | async-start | bytes 4194304 | tf_op jit(solution)/shard_map/all_to_all | solution.py:111
  80.7 66.2 %copy-start.1 = (bf16[512,2048]{1,0:T(8,128)(2,1)S(1)}, bf16[512,2048]{1,0:T(8,128)(2,1)}, u32[]{:S(2)}) copy-start(bf16[512,2048]{1,0:T(8,128)(2,1)} %copy.27) | copy-start | bytes 6291460
  223.8 57.5 %all-to-all-start.1 = ((f32[2048,2,2,128]{3,2,1,0:T(2,128)}), f32[2048,2,2,128]{3,2,1,0:T(2,128)}, u32[]{:S(2)}, u32[]{:S(2)}) async-start(f32[2048,2,2,128]{3,2,1,0:T(2,128)} %copy.28), calls=%async_computation.1 | async-start | bytes 8388608 | tf_op jit(solution)/shard_map/all_to_all | solution.py:113
  228.7 126.9 %all-reduce.2.cloned.1.call-start = ((), (), s32[]{:S(2)}) async-start(), calls=%async_computation.2 | async-start | bytes 4194304 | tf_op jit(solution)/shard_map/psum | solution.py:16
  292.9 3.3 copy-start.2
  292.9 4.5 copy-start.3
  355.6 2.8 copy-start
Sparse Core Ops, SparseCore 0:
  296.3 59.2 all-reduce.1
where the time goes:
time: 534 us; the launch traced here: 527 us
  matrix products  196 us (37%)
  waiting for transfers between devices  130 us (24%)
  local copies, waits for them, and re-layouts  93.7 us (18%)
  blocking collectives  64.9 us (12%)
  other arithmetic  15.2 us (3%)
  between operations  13.8 us (3%)
  starting transfers between devices  13.3 us (2%)
    dot_general x1, matrix products, transform(): jnp.dot(sin_table, flat, preferred_element_type=jnp.float32)  66.2 us
    psum x1, blocking collectives, body(): total = lax.psum(partial_bins, ('field', 'gz'))  64.9 us
    dot_general x1, matrix products, transform(): jnp.dot(cos_table, flat, preferred_element_type=jnp.float32)  63.9 us
    psum x1, waiting for transfers between devices, broadcast(): return lax.psum(kept, axis)  54.6 us
    all_to_all x1, waiting for transfers between devices, body(): lax.all_to_all(spectra_lines, 'gz', split_axis=0, concat_axis=3, tiled=True)  46.7 us
    dot_general x8, matrix products, step(): lax.dot_general(rows, shell_hot, (((1,), (1,)), ((), ())), preferred_elem...  44.1 us
    all_to_all x1, waiting for transfers between devices, body(): lax.all_to_all(own, 'gz', split_axis=3, concat_axis=0, tiled=True)  28.8 us
    unnamed x13, local copies, waits for them, and re-layouts  26.5 us
  transfers between devices with their start and end apart: 3, of which 3 were waited for; matrix products, arithmetic and copies ran while one was open for 2% of the time, Pallas kernels for 0%

commit v1 on v0

v1 whole, which is shorter than its diff:
```python
import math

import jax
import jax.numpy as jnp
import numpy as np
from jax import lax
from jax.experimental import pallas as pl
from jax.experimental.pallas import tpu as pltpu
from jax.sharding import PartitionSpec as P

NZ = 2048
HALF = NZ // 2
SHELLS = 256
MUBINS = 8
PLANES = 16
YROWS = 256
COLS = 32
ROWS = 72
TK = 256
BOTH = ("field", "gz")


def dft_tables():
    index = np.arange(NZ, dtype=np.int64)
    product = (np.arange(HALF + 1, dtype=np.int64)[:, None] * index[None, :]) % NZ
    angle = (product.astype(np.float32) * np.float32(2.0 * math.pi / NZ)).astype(np.float64)
    factor = np.float32(1.0 / math.sqrt(NZ))
    cos_rows = (np.cos(angle).astype(np.float32) * factor).astype(jnp.bfloat16)
    sin_rows = (np.sin(angle).astype(np.float32) * factor).astype(jnp.bfloat16)
    sin_rows[0] = cos_rows[HALF]
    return cos_rows[:HALF], sin_rows[:HALF]


def swap_groups(parts, lane):
    upper = lane >= 64
    odd = (lane & 32) != 0
    a, b, c, d = parts
    a, c = jnp.where(upper, pltpu.roll(c, 64, 1), a), jnp.where(upper, c, pltpu.roll(a, 64, 1))
    b, d = jnp.where(upper, pltpu.roll(d, 64, 1), b), jnp.where(upper, d, pltpu.roll(b, 64, 1))
    a, b = jnp.where(odd, pltpu.roll(b, 32, 1), a), jnp.where(odd, b, pltpu.roll(a, 96, 1))
    c, d = jnp.where(odd, pltpu.roll(d, 32, 1), c), jnp.where(odd, d, pltpu.roll(c, 96, 1))
    return a, b, c, d


def pack_kernel(place, fields_ref, shells_ref, mubins_ref, out_ref):
    step = pl.program_id(0)
    row = lax.broadcasted_iota(jnp.int32, (256, 256), 0)
    col = lax.broadcasted_iota(jnp.int32, (256, 256), 1)
    lane = lax.broadcasted_iota(jnp.int32, (256, 128), 1)
    order = (col == (row % 16) * 16 + row // 16).astype(jnp.bfloat16)
    parts = [
        jnp.dot(
            order,
            fields_ref[:, c, f].reshape(256, YROWS),
            preferred_element_type=jnp.float32,
        )
        for c in range(2)
        for f in range(2)
    ]
    start = pl.multiple_of(step * 16, 16)
    for half in range(2):
        quarters = swap_groups([part[:, half * 128 : half * 128 + 128] for part in parts], lane)
        for q in range(4):
            block = quarters[q].astype(jnp.bfloat16).reshape(16, 16, 128)
            for p in range(PLANES):
                out_ref[q * 32 + p * 2 + half, pl.ds(start, 16), :] = block[p]

    @pl.when(step == 3)
    def _():
        inner = row % 16
        inner = jnp.where(place[1] >= 16, 15 - inner, inner)
        turned = (col == inner * 16 + row // 16).astype(jnp.bfloat16)
        maps = [
            jnp.dot(
                turned,
                ref[...].reshape(256, YROWS).astype(jnp.bfloat16),
                preferred_element_type=jnp.float32,
            ).reshape(16, 2, 8, YROWS)
            for ref in (shells_ref, mubins_ref)
        ]
        groups = [item[:, h].reshape(128, YROWS) for item in maps for h in range(2)]
        for half in range(2):
            quarters = swap_groups([g[:, half * 128 : half * 128 + 128] for g in groups], lane[:128])
            for q in range(4):
                block = quarters[q].reshape(16, 8, 128)
                for p in range(PLANES):
                    out_ref[q * 32 + p * 2 + half, 64:72, :] = block[p].astype(jnp.bfloat16)


def pack(place, fields, shells, mubins):
    return pl.pallas_call(
        pack_kernel,
        grid_spec=pltpu.PrefetchScalarGridSpec(
            num_scalar_prefetch=1,
            grid=(4,),
            in_specs=[
                pl.BlockSpec((16, 2, 2, PLANES, YROWS), lambda i, place: (i, 0, 0, 0, 0)),
                pl.BlockSpec((16, PLANES, YROWS), lambda i, place: (place[2], 0, 0)),
                pl.BlockSpec((16, PLANES, YROWS), lambda i, place: (place[2], 0, 0)),
            ],
            out_specs=pl.BlockSpec((128, ROWS, 128), lambda i, place: (0, 0, 0)),
        ),
        out_shape=jax.ShapeDtypeStruct((128, ROWS, 128), jnp.bfloat16),
        compiler_params=pltpu.CompilerParams(vmem_limit_bytes=32 * 1024 * 1024),
        name="pack",
    )(place, fields, shells, mubins)


def fold(parts, lane, width):
    first, second = parts
    odd = (lane & width) != 0
    kept = jnp.where(odd, second, first)
    moved = jnp.where(odd, first, second)
    return kept + pltpu.roll(moved, width, 1) if width == 64 else kept + swap32(moved, lane)


def swap32(value, lane):
    odd = (lane & 32) != 0
    return jnp.where(odd, pltpu.roll(value, 32, 1), pltpu.roll(value, 96, 1))


def bins_kernel(place, recv_ref, cos_ref, sin_ref, out_ref, lines, low, high, real, turn, values, hot_v, hot_s, acc):
    step = pl.program_id(0)
    lane = lax.broadcasted_iota(jnp.int32, (8, 128), 1)
    sub = lax.broadcasted_iota(jnp.int32, (8, 128), 0)
    upper = lane >= 64
    odd = (lane & 32) != 0

    @pl.when(step == 0)
    def _():
        acc[...] = jnp.zeros_like(acc)
        for f in range(4):
            for j in range(32):
                lines[j * 64 : j * 64 + 64, f * 128 : f * 128 + 128] = recv_ref[f * 32 + j, 0:64, :]
        tiles = []
        for tile in range(64):
            turned = tile >= 32
            source = 31 - (tile - 32) // 2 if turned else tile // 2
            pair = (tile % 2) * 2
            one = recv_ref[pair * 32 + source, 64:72, :].astype(jnp.float32)
            two = recv_ref[(pair + 1) * 32 + source, 64:72, :].astype(jnp.float32)
            shell = jnp.where(upper, pltpu.roll(two, 64, 1), one)
            mu = jnp.where(upper, two, pltpu.roll(one, 64, 1))
            tiles.append(shell + 256.0 * mu)
        rolled = [pltpu.roll(t, 1, 0) for t in tiles[32:]]
        moved = [pltpu.roll(t, 32, 1) for t in rolled]
        for m in range(32):
            first = jnp.where(lane < 32, moved[m - 1], moved[m])
            tiles[32 + m] = jnp.where(sub == 0, first, rolled[m])
        for tile in range(64):
            top = jnp.floor(tiles[tile] * (1.0 / 128.0))
            at = ((tile % 32) * 2 + tile // 32) * 8
            high[at : at + 8, :] = top
            low[at : at + 8, :] = tiles[tile] - 128.0 * top

    real[...] = jnp.dot(cos_ref[...], lines[...], preferred_element_type=jnp.float32)
    turn[...] = jnp.dot(sin_ref[...], lines[...], preferred_element_type=jnp.float32)

    spot = place[1]
    col = (lane & 31).astype(jnp.float32)
    wave_x = (NZ // 4 + spot // 2).astype(jnp.float32)
    wave_y = (NZ // 8 + (spot % 2) * 128 + place[0] * 32).astype(jnp.float32) + col
    plane_square = wave_x * wave_x + wave_y * wave_y
    weight_one = jnp.where(odd, wave_y * wave_y, wave_x * wave_x) * 1.5
    mixed = wave_x * wave_y * 3.0
    linear = jnp.where(odd, wave_y, wave_x) * 3.0
    turn_sign = jnp.where(upper, -1.0, 1.0)
    step16 = lax.broadcasted_iota(jnp.int32, (16, 128), 0).astype(jnp.float32).astype(jnp.bfloat16)
    step128 = lax.broadcasted_iota(jnp.int32, (128, 128), 0).astype(jnp.float32).astype(jnp.bfloat16)

    def tile_body(m, carry):
        products = [[], []]
        for q in range(4):
            at = pl.multiple_of(m * 32 + q * 8, 8)
            k_row = step * TK + at + sub
            first = k_row == 0
            wave_z = k_row.astype(jnp.float32)
            for sign in range(2):
                kz = wave_z if sign == 0 else jnp.where(first, -float(HALF), -wave_z)
                square = kz * kz
                inverse = 1.0 / (plane_square + square)
                weights = (
                    None,
                    weight_one * inverse,
                    jnp.where(odd, mixed, 1.5 * square) * inverse,
                    linear * kz * inverse,
                )
                spectra = []
                for f in range(4):
                    a = real[pl.ds(at, 8), f * 128 : f * 128 + 128]
                    b = pltpu.roll(turn[pl.ds(at, 8), f * 128 : f * 128 + 128], 64, 1) * turn_sign
                    if sign == 0:
                        spectra.append(a + jnp.where(first, 0.0, b))
                    else:
                        spectra.append(jnp.where(first, 0.0, a) - b)
                base = jnp.where(odd, pltpu.roll(spectra[0], 32, 1), spectra[0])
                cross = [base * s for s in spectra]
                products[sign].append([cross[0]] + [cross[f] * weights[f] for f in (1, 2, 3)])
        for sign in range(2):
            quad = products[sign]
            pairs = [
                (fold((quad[0][f], quad[2][f]), lane, 64), fold((quad[1][f], quad[3][f]), lane, 64))
                for f in range(4)
            ]
            even, other = pairs[0]
            tiles = [
                jnp.where(odd, pltpu.roll(other, 32, 1), even),
                jnp.where(odd, other, pltpu.roll(even, 96, 1)),
            ] + [fold(pairs[f], lane, 32) for f in (1, 2, 3)]
            at = pl.multiple_of((step * (TK // 32) + m) * 16 + sign * 8, 8)
            lows = low[pl.ds(at, 8), :]
            highs = high[pl.ds(at, 8), :]
            for r in range(8):
                place_at = (sign * 8 + r) * 128
                spread = jnp.broadcast_to(highs[r : r + 1], (16, 128)).astype(jnp.bfloat16)
                hit = spread == step16
                for v in range(5):
                    item = jnp.broadcast_to(tiles[v][r : r + 1], (16, 128)).astype(jnp.bfloat16)
                    hot_v[v * 16 : v * 16 + 16, place_at : place_at + 128] = jnp.where(
                        hit, item, jnp.bfloat16(0)
                    )
                hot_v[80:96, place_at : place_at + 128] = jnp.where(hit, jnp.bfloat16(1), jnp.bfloat16(0))
                spread = jnp.broadcast_to(lows[r : r + 1], (16, 128)).astype(jnp.bfloat16)
                spread = jnp.concatenate([spread] * 8, axis=0)
                hot_s[:, place_at : place_at + 128] = jnp.where(
                    spread == step128, jnp.bfloat16(1), jnp.bfloat16(0)
                )
        acc[...] += lax.dot_general(
            hot_v[...], hot_s[...], (((1,), (1,)), ((), ())), preferred_element_type=jnp.float32
        )
        return carry

    lax.fori_loop(0, TK // 32, tile_body, 0)

    @pl.when(step == pl.num_programs(0) - 1)
    def _():
        out_ref[0:32, :] = acc[0:32, :]
        out_ref[32:48, :] = acc[32:48, :] + acc[48:64, :] + acc[64:80, :] - 0.5 * acc[16:32, :]
        out_ref[48:64, :] = acc[80:96, :]


def bins(place, received, cos_table, sin_table):
    return pl.pallas_call(
        bins_kernel,
        grid_spec=pltpu.PrefetchScalarGridSpec(
            num_scalar_prefetch=1,
            grid=(HALF // TK,),
            in_specs=[
                pl.BlockSpec((128, ROWS, 128), lambda i, place: (0, 0, 0)),
                pl.BlockSpec((TK, NZ), lambda i, place: (i, 0)),
                pl.BlockSpec((TK, NZ), lambda i, place: (i, 0)),
            ],
            out_specs=pl.BlockSpec((64, 128), lambda i, place: (0, 0)),
            scratch_shapes=[
                pltpu.VMEM((NZ, 512), jnp.bfloat16),
                pltpu.VMEM((512, 128), jnp.float32),
                pltpu.VMEM((512, 128), jnp.float32),
                pltpu.VMEM((TK, 512), jnp.float32),
                pltpu.VMEM((TK, 512), jnp.float32),
                pltpu.VMEM((8, 128), jnp.float32),
                pltpu.VMEM((96, 2048), jnp.bfloat16),
                pltpu.VMEM((128, 2048), jnp.bfloat16),
                pltpu.VMEM((96, 128), jnp.float32),
            ],
        ),
        out_shape=jax.ShapeDtypeStruct((64, 128), jnp.float32),
        compiler_params=pltpu.CompilerParams(vmem_limit_bytes=40 * 1024 * 1024),
        name="bins",
    )(place, received, cos_table, sin_table)


def total_over_devices(value):
    for axis, size, bit in (
        ("gz", 32, 1),
        ("gz", 32, 2),
        ("gz", 32, 8),
        ("field", 4, 1),
        ("gz", 32, 6),
        ("gz", 32, 24),
        ("field", 4, 3),
    ):
        value = value + lax.ppermute(value, axis, [(i, i ^ bit) for i in range(size)])
    return value


def body(fields, shells, mubins):
    field, spot = lax.axis_index("field"), lax.axis_index("gz")
    cos_table, sin_table = dft_tables()
    place = jnp.stack([field, spot, jnp.where(spot >= 16, 3 - field, field)]).astype(jnp.int32)
    sent = pack(place, fields, shells, mubins)
    received = lax.all_to_all(sent, BOTH, split_axis=0, concat_axis=0, tiled=True)
    partial = bins(place, received, jnp.asarray(cos_table), jnp.asarray(sin_table))
    total = total_over_devices(partial).reshape(4, MUBINS, SHELLS)
    return total[:3] / jnp.maximum(total[3], 1.0)[None]


def solution(mesh):
    in_specs = (P("gz", None, "field", None, None), P("gz", None, None), P("gz", None, None))
    return jax.shard_map(body, mesh=mesh, in_specs=in_specs, out_specs=P(), check_vma=False)
```

time: 534 us -> 108 us (0.20); the launches traced: 527 us -> 108 us
  matrix products: 196 us -> 0 us
  waiting for transfers between devices: 130 us -> 25.2 us
  local copies, waits for them, and re-layouts: 93.7 us -> 4.07 us
  Pallas kernels: 0 us -> 29.9 us
  blocking collectives: 64.9 us -> 44.4 us
  other arithmetic: 15.2 us -> 0.74 us
  between operations: 13.8 us -> 0.07 us
  starting transfers between devices: 13.3 us -> 3.23 us
    dot_general x11 -> x0, matrix products: 196 us -> none  [the longest x1 66.2 us: transform(): jnp.dot(sin_table, flat, preferred_element_type=jnp.float32)]
    all_to_all x2 -> x0, waiting for transfers between devices: 75.6 us -> none  [the longest x1 46.7 us: body(): lax.all_to_all(spectra_lines, 'gz', split_axis=0, concat_axis=3, tiled=True)]
    psum x1 -> x0, blocking collectives: 64.9 us -> none  [body(): total = lax.psum(partial_bins, ('field', 'gz'))]
    psum x1 -> x0, waiting for transfers between devices: 54.6 us -> none  [broadcast(): return lax.psum(kept, axis)]
    all_to_all x0 -> x1, blocking collectives: none -> 44.4 us  [body(): lax.all_to_all(sent, BOTH, split_axis=0, concat_axis=0, tiled=True)]
    pallas_call x0 -> x2, Pallas kernels: none -> 29.9 us  [the longest x1 26.9 us: bins(): pl.pallas_call(bins_kernel, grid_spec=pltpu.PrefetchScalarGridSpec(num_sc...]
    ppermute x0 -> x7, waiting for transfers between devices: none -> 25.2 us  [total_over_devices(): lax.ppermute(value, axis, [(i, i ^ bit) for i in range(size)])]
    unnamed x13 -> x10, local copies, waits for them, and re-layouts: 26.5 us -> 4.05 us
  transfers between devices with their start and end apart: 3 -> 7, of which waited for: 3 -> 7; matrix products, arithmetic and copies ran while one was open for 2% -> 0% of each run, Pallas kernels for 0% -> 0%
where the time goes in v1:
time: 108 us
  blocking collectives  44.4 us (41%)
  Pallas kernels  29.9 us (28%)
  waiting for transfers between devices  25.2 us (23%)
  local copies, waits for them, and re-layouts  4.07 us (4%)
  starting transfers between devices  3.23 us (3%)
    all_to_all x1, blocking collectives, body(): lax.all_to_all(sent, BOTH, split_axis=0, concat_axis=0, tiled=True)  44.4 us
    pallas_call x1, Pallas kernels, bins(): pl.pallas_call(bins_kernel, grid_spec=pltpu.PrefetchScalarGridSpec(num_sc...  26.9 us
    ppermute x7, waiting for transfers between devices, total_over_devices(): lax.ppermute(value, axis, [(i, i ^ bit) for i in range(size)])  25.2 us
    unnamed x10, local copies, waits for them, and re-layouts  4.05 us
    ppermute x7, starting transfers between devices, total_over_devices(): lax.ppermute(value, axis, [(i, i ^ bit) for i in range(size)])  3.23 us
    pallas_call x1, Pallas kernels, pack(): pl.pallas_call(pack_kernel, grid_spec=pltpu.PrefetchScalarGridSpec(num_sc...  3.07 us
  transfers between devices with their start and end apart: 7, of which 7 were waited for; matrix products, arithmetic and copies ran while one was open for 0% of the time, Pallas kernels for 0%

profile of v1, /device:TPU:0, one launch (start us, length us, event | category | flops | bytes accessed | tf_op | source)
XLA Modules:
  0.0 107.6 jit_solution(2923022083600618570)
XLA Ops:
  0.0 0.1 pad_add_fusion.place
  0.1 0.0 copy-start.2
  0.1 1.6 %copy-done.2 = bf16[64,2,2,16,256]{4,3,2,1,0:T(8,128)(2,1)S(1)} copy-done((bf16[64,2,2,16,256]{4,3,2,1,0:T(8,128)(2,1)S(1)}, bf16[64,2,2,16,256]{4,3,2,1,0:T(8,128)(2,1)}, u32[]{:S(2)}) %copy-start.2) | copy-done | bytes 2097176
  1.7 0.0 copy-start.3
  1.7 1.2 %copy-done.3 = s32[64,16,256]{2,1,0:T(8,128)S(1)} copy-done((s32[64,16,256]{2,1,0:T(8,128)S(1)}, s32[64,16,256]{2,1,0:T(8,128)}, u32[]{:S(2)}) %copy-start.3) | copy-done | bytes 1048600
  2.9 0.0 copy-start.4
  2.9 1.2 %copy-done.4 = s32[64,16,256]{2,1,0:T(8,128)S(1)} copy-done((s32[64,16,256]{2,1,0:T(8,128)S(1)}, s32[64,16,256]{2,1,0:T(8,128)}, u32[]{:S(2)}) %copy-start.4) | copy-done | bytes 1048600
  4.1 0.0 copy-start.1
  4.1 3.1 %pack.1 = bf16[128,72,128]{2,1,0:T(8,128)(2,1)S(1)} custom-call(s32[3]{0:T(128)S(1)} %pad_add_fusion.place, bf16[64,2,2,16,256]{4,3,2,1,0:T(8,128)(2,1)S(1)} %copy-done.2, s32[64,16,256]{2,1,0:T(8,128)S(1)} %copy-done.3, s32[64,16,256]{2,1,0:T(8,128)S(1)} %copy-done.4), custom_call_target="tpu_custom_call" | custom-call | tf_op jit(solution)/shard_map/pack/pallas_call | solution.py:91
  7.2 0.0 copy-start
  7.2 44.4 %all_to_all.5.recv_ref = bf16[128,72,128]{2,1,0:T(8,128)(2,1)S(1)} all-to-all(bf16[128,72,128]{2,1,0:T(8,128)(2,1)S(1)} %pack.1), channel_id=1, replica_groups=mesh['field'=4,'gz'=32] {'field','gz'}, dimensions={0} | all-to-all | bytes 4718592 | tf_op jit(solution)/shard_map/all_to_all | solution.py:291
  51.6 0.0 copy-done.1
  51.6 0.0 copy-done
  51.6 26.9 %bins.1 = f32[64,128]{1,0:T(8,128)S(1)} custom-call(s32[3]{0:T(128)S(1)} %pad_add_fusion.place, bf16[128,72,128]{2,1,0:T(8,128)(2,1)S(1)} %all_to_all.5.recv_ref, bf16[1024,2048]{1,0:T(8,128)(2,1)S(1)} %copy-done.1, bf16[1024,2048]{1,0:T(8,128)(2,1)S(1)} %copy-done), custom_call_target="tpu_custom_call" | custom-call | tf_op jit(solution)/shard_map/bins/pallas_call | solution.py:243
  78.5 0.1 collective-permute-start
  78.6 1.2 %collective-permute-done = f32[64,128]{1,0:T(8,128)S(1)} collective-permute-done((f32[64,128]{1,0:T(8,128)S(1)}, f32[64,128]{1,0:T(8,128)S(1)}, u32[]{:S(2)}, u32[]{:S(2)}) %collective-permute-start) | collective-permute-done | bytes 32800 | tf_op jit(solution)/shard_map/ppermute | solution.py:282
  79.8 0.2 collective-permute-start.1
  80.0 3.7 %collective-permute-done.1 = f32[64,128]{1,0:T(8,128)S(1)} collective-permute-done((f32[64,128]{1,0:T(8,128)S(1)}, f32[64,128]{1,0:T(8,128)S(1)}, u32[]{:S(2)}, u32[]{:S(2)}) %collective-permute-start.1) | collective-permute-done | bytes 32800 | tf_op jit(solution)/shard_map/ppermute | solution.py:282
  83.7 0.4 collective-permute-start.2
  84.1 3.5 %collective-permute-done.2 = f32[64,128]{1,0:T(8,128)S(1)} collective-permute-done((f32[64,128]{1,0:T(8,128)S(1)}, f32[64,128]{1,0:T(8,128)S(1)}, u32[]{:S(2)}, u32[]{:S(2)}) %collective-permute-start.2) | collective-permute-done | bytes 32800 | tf_op jit(solution)/shard_map/ppermute | solution.py:282
  87.6 0.6 collective-permute-start.3
  88.2 3.3 %collective-permute-done.3 = f32[64,128]{1,0:T(8,128)S(1)} collective-permute-done((f32[64,128]{1,0:T(8,128)S(1)}, f32[64,128]{1,0:T(8,128)S(1)}, u32[]{:S(2)}, u32[]{:S(2)}) %collective-permute-start.3) | collective-permute-done | bytes 32800 | tf_op jit(solution)/shard_map/ppermute | solution.py:282
  91.5 0.2 collective-permute-start.4
  91.7 5.0 %collective-permute-done.4 = f32[64,128]{1,0:T(8,128)S(1)} collective-permute-done((f32[64,128]{1,0:T(8,128)S(1)}, f32[64,128]{1,0:T(8,128)S(1)}, u32[]{:S(2)}, u32[]{:S(2)}) %collective-permute-start.4) | collective-permute-done | bytes 32800 | tf_op jit(solution)/shard_map/ppermute | solution.py:282
  96.7 0.6 collective-permute-start.5
  97.3 4.5 %collective-permute-done.5 = f32[64,128]{1,0:T(8,128)S(1)} collective-permute-done((f32[64,128]{1,0:T(8,128)S(1)}, f32[64,128]{1,0:T(8,128)S(1)}, u32[]{:S(2)}, u32[]{:S(2)}) %collective-permute-start.5) | collective-permute-done | bytes 32800 | tf_op jit(solution)/shard_map/ppermute | solution.py:282
  101.8 1.1 %collective-permute-start.6 = (f32[64,128]{1,0:T(8,128)S(1)}, f32[64,128]{1,0:T(8,128)S(1)}, u32[]{:S(2)}, u32[]{:S(2)}) collective-permute-start(f32[64,128]{1,0:T(8,128)S(1)} %add.26), channel_id=1, source_target_pairs={{0,96},{32,64},{64,32},{96,0},{1,97},{33,65},{65,33},{97,1},{2,98}... | collective-permute-start | bytes 98312 | tf_op jit(solution)/shard_map/ppermute | solution.py:282
  102.9 4.0 %collective-permute-done.6 = f32[64,128]{1,0:T(8,128)S(1)} collective-permute-done((f32[64,128]{1,0:T(8,128)S(1)}, f32[64,128]{1,0:T(8,128)S(1)}, u32[]{:S(2)}, u32[]{:S(2)}) %collective-permute-start.6) | collective-permute-done | bytes 32800 | tf_op jit(solution)/shard_map/ppermute | solution.py:282
  107.0 0.6 broadcast_divide_fusion
  (11 shorter events, 0.1 us)
Async XLA Ops:
  0.1 1.6 %copy-start.2 = (bf16[64,2,2,16,256]{4,3,2,1,0:T(8,128)(2,1)S(1)}, bf16[64,2,2,16,256]{4,3,2,1,0:T(8,128)(2,1)}, u32[]{:S(2)}) copy-start(bf16[64,2,2,16,256]{4,3,2,1,0:T(8,128)(2,1)} %fields_ref.1) | copy-start | bytes 6291460
  1.7 1.2 %copy-start.3 = (s32[64,16,256]{2,1,0:T(8,128)S(1)}, s32[64,16,256]{2,1,0:T(8,128)}, u32[]{:S(2)}) copy-start(s32[64,16,256]{2,1,0:T(8,128)} %shells_ref.1) | copy-start | bytes 3145732
  2.9 1.2 %copy-start.4 = (s32[64,16,256]{2,1,0:T(8,128)S(1)}, s32[64,16,256]{2,1,0:T(8,128)}, u32[]{:S(2)}) copy-start(s32[64,16,256]{2,1,0:T(8,128)} %mubins_ref.1) | copy-start | bytes 3145732
  4.1 47.5 %copy-start.1 = (bf16[1024,2048]{1,0:T(8,128)(2,1)S(1)}, bf16[1024,2048]{1,0:T(8,128)(2,1)}, u32[]{:S(2)}) copy-start(bf16[1024,2048]{1,0:T(8,128)(2,1)} %constant.19.clone.cos_ref) | copy-start | bytes 12582916
  7.2 44.4 %copy-start = (bf16[1024,2048]{1,0:T(8,128)(2,1)S(1)}, bf16[1024,2048]{1,0:T(8,128)(2,1)}, u32[]{:S(2)}) copy-start(bf16[1024,2048]{1,0:T(8,128)(2,1)} %constant.20.clone.sin_ref) | copy-start | bytes 12582916
  78.5 1.3 %collective-permute-start = (f32[64,128]{1,0:T(8,128)S(1)}, f32[64,128]{1,0:T(8,128)S(1)}, u32[]{:S(2)}, u32[]{:S(2)}) collective-permute-start(f32[64,128]{1,0:T(8,128)S(1)} %bins.1), channel_id=1, source_target_pairs={{0,1},{1,0},{2,3},{3,2},{4,5},{5,4},{6,7},{7,6},{8,9},{9,8},{10,11... | collective-permute-start | bytes 98312 | tf_op jit(solution)/shard_map/ppermute | solution.py:282
  79.8 3.9 %collective-permute-start.1 = (f32[64,128]{1,0:T(8,128)S(1)}, f32[64,128]{1,0:T(8,128)S(1)}, u32[]{:S(2)}, u32[]{:S(2)}) collective-permute-start(f32[64,128]{1,0:T(8,128)S(1)} %add.21), channel_id=1, source_target_pairs={{0,2},{1,3},{2,0},{3,1},{4,6},{5,7},{6,4},{7,5},{8,10},{9,11},{10,... | collective-permute-start | bytes 98312 | tf_op jit(solution)/shard_map/ppermute | solution.py:282
  83.7 3.9 %collective-permute-start.2 = (f32[64,128]{1,0:T(8,128)S(1)}, f32[64,128]{1,0:T(8,128)S(1)}, u32[]{:S(2)}, u32[]{:S(2)}) collective-permute-start(f32[64,128]{1,0:T(8,128)S(1)} %add.22), channel_id=1, source_target_pairs={{0,8},{1,9},{2,10},{3,11},{4,12},{5,13},{6,14},{7,15},{8,0},{9,1},... | collective-permute-start | bytes 98312 | tf_op jit(solution)/shard_map/ppermute | solution.py:282
  87.6 3.9 %collective-permute-start.3 = (f32[64,128]{1,0:T(8,128)S(1)}, f32[64,128]{1,0:T(8,128)S(1)}, u32[]{:S(2)}, u32[]{:S(2)}) collective-permute-start(f32[64,128]{1,0:T(8,128)S(1)} %add.23), channel_id=1, source_target_pairs={{0,32},{32,0},{64,96},{96,64},{1,33},{33,1},{65,97},{97,65},{2,34}... | collective-permute-start | bytes 98312 | tf_op jit(solution)/shard_map/ppermute | solution.py:282
  91.5 5.1 %collective-permute-start.4 = (f32[64,128]{1,0:T(8,128)S(1)}, f32[64,128]{1,0:T(8,128)S(1)}, u32[]{:S(2)}, u32[]{:S(2)}) collective-permute-start(f32[64,128]{1,0:T(8,128)S(1)} %add.24), channel_id=1, source_target_pairs={{0,6},{1,7},{2,4},{3,5},{4,2},{5,3},{6,0},{7,1},{8,14},{9,15},{10,... | collective-permute-start | bytes 98312 | tf_op jit(solution)/shard_map/ppermute | solution.py:282
  96.7 5.1 %collective-permute-start.5 = (f32[64,128]{1,0:T(8,128)S(1)}, f32[64,128]{1,0:T(8,128)S(1)}, u32[]{:S(2)}, u32[]{:S(2)}) collective-permute-start(f32[64,128]{1,0:T(8,128)S(1)} %add.25), channel_id=1, source_target_pairs={{0,24},{1,25},{2,26},{3,27},{4,28},{5,29},{6,30},{7,31},{8,16},{9,... | collective-permute-start | bytes 98312 | tf_op jit(solution)/shard_map/ppermute | solution.py:282
  101.8 5.1 %collective-permute-start.6 = (f32[64,128]{1,0:T(8,128)S(1)}, f32[64,128]{1,0:T(8,128)S(1)}, u32[]{:S(2)}, u32[]{:S(2)}) collective-permute-start(f32[64,128]{1,0:T(8,128)S(1)} %add.26), channel_id=1, source_target_pairs={{0,96},{32,64},{64,32},{96,0},{1,97},{33,65},{65,33},{97,1},{2,98}... | collective-permute-start | bytes 98312 | tf_op jit(solution)/shard_map/ppermute | solution.py:282

commit v2 on v1

v2 whole, which is shorter than its diff:
```python
import math

import jax
import jax.numpy as jnp
import numpy as np
from jax import lax
from jax.experimental import pallas as pl
from jax.experimental.pallas import tpu as pltpu
from jax.sharding import PartitionSpec as P

NZ = 2048
HALF = NZ // 2
SHELLS = 256
MUBINS = 8
PLANES = 16
YROWS = 256
COLS = 32
ROWS = 72
TK = 256
UNROLL = 8
BOTH = ("field", "gz")


def dft_tables():
    index = np.arange(NZ, dtype=np.int64)
    product = (np.arange(HALF + 1, dtype=np.int64)[:, None] * index[None, :]) % NZ
    angle = (product.astype(np.float32) * np.float32(2.0 * math.pi / NZ)).astype(np.float64)
    factor = np.float32(1.0 / math.sqrt(NZ))
    cos_rows = (np.cos(angle).astype(np.float32) * factor).astype(jnp.bfloat16)
    sin_rows = (np.sin(angle).astype(np.float32) * factor).astype(jnp.bfloat16)
    sin_rows[0] = cos_rows[HALF]
    return cos_rows[:HALF], sin_rows[:HALF]


def swap_groups(parts, lane):
    upper = lane >= 64
    odd = (lane & 32) != 0
    a, b, c, d = parts
    a, c = jnp.where(upper, pltpu.roll(c, 64, 1), a), jnp.where(upper, c, pltpu.roll(a, 64, 1))
    b, d = jnp.where(upper, pltpu.roll(d, 64, 1), b), jnp.where(upper, d, pltpu.roll(b, 64, 1))
    a, b = jnp.where(odd, pltpu.roll(b, 32, 1), a), jnp.where(odd, b, pltpu.roll(a, 96, 1))
    c, d = jnp.where(odd, pltpu.roll(d, 32, 1), c), jnp.where(odd, d, pltpu.roll(c, 96, 1))
    return a, b, c, d


def pack_kernel(place, fields_hbm, shells_hbm, mubins_hbm, out_ref, fields_ref, index_ref, field_sems, index_sems):
    spot = pl.multiple_of(place[2] * 16, 16)
    copies = [
        pltpu.make_async_copy(
            fields_hbm.at[pl.ds(part * 16, 16)], fields_ref.at[pl.ds(part * 16, 16)], field_sems.at[part]
        )
        for part in range(4)
    ]
    index_copies = [
        pltpu.make_async_copy(source.at[pl.ds(spot, 16)], index_ref.at[n], index_sems.at[n])
        for n, source in enumerate((shells_hbm, mubins_hbm))
    ]
    for copy in index_copies + copies:
        copy.start()
    row = lax.broadcasted_iota(jnp.int32, (256, 256), 0)
    col = lax.broadcasted_iota(jnp.int32, (256, 256), 1)
    lane = lax.broadcasted_iota(jnp.int32, (256, 128), 1)
    inner = row % 16
    order = (col == inner * 16 + row // 16).astype(jnp.bfloat16)
    turned = jnp.where(place[1] >= 16, 15 - inner, inner)
    turned = (col == turned * 16 + row // 16).astype(jnp.bfloat16)

    for copy in index_copies:
        copy.wait()
    maps = [
        jnp.dot(
            turned,
            index_ref[n].reshape(256, YROWS).astype(jnp.bfloat16),
            preferred_element_type=jnp.float32,
        ).reshape(16, 2, 8, YROWS)
        for n in range(2)
    ]
    groups = [item[:, h].reshape(128, YROWS) for item in maps for h in range(2)]
    for half in range(2):
        quarters = swap_groups([g[:, half * 128 : half * 128 + 128] for g in groups], lane[:128])
        for q in range(4):
            block = quarters[q].reshape(16, 8, 128)
            for p in range(PLANES):
                out_ref[q * 32 + p * 2 + half, 64:72, :] = block[p].astype(jnp.bfloat16)

    for part in range(4):
        copies[part].wait()
        start = part * 16
        parts = [
            jnp.dot(
                order,
                fields_ref[start : start + 16, c, f].reshape(256, YROWS),
                preferred_element_type=jnp.float32,
            )
            for c in range(2)
            for f in range(2)
        ]
        for half in range(2):
            quarters = swap_groups([item[:, half * 128 : half * 128 + 128] for item in parts], lane)
            for q in range(4):
                block = quarters[q].astype(jnp.bfloat16).reshape(16, 16, 128)
                for p in range(PLANES):
                    out_ref[q * 32 + p * 2 + half, start : start + 16, :] = block[p]


def pack(place, fields, shells, mubins):
    return pl.pallas_call(
        pack_kernel,
        in_specs=[pl.BlockSpec(memory_space=pltpu.SMEM)] + [pl.BlockSpec(memory_space=pltpu.HBM)] * 3,
        out_specs=pl.BlockSpec(memory_space=pltpu.VMEM),
        scratch_shapes=[
            pltpu.VMEM((64, 2, 2, PLANES, YROWS), jnp.bfloat16),
            pltpu.VMEM((2, 16, PLANES, YROWS), jnp.int32),
            pltpu.SemaphoreType.DMA((4,)),
            pltpu.SemaphoreType.DMA((2,)),
        ],
        out_shape=jax.ShapeDtypeStruct((128, ROWS, 128), jnp.bfloat16),
        compiler_params=pltpu.CompilerParams(vmem_limit_bytes=32 * 1024 * 1024),
        name="pack",
    )(place, *[pltpu.with_memory_space_constraint(x, pltpu.HBM) for x in (fields, shells, mubins)])


def fold(parts, lane, width):
    first, second = parts
    odd = (lane & width) != 0
    kept = jnp.where(odd, second, first)
    moved = jnp.where(odd, first, second)
    return kept + pltpu.roll(moved, width, 1) if width == 64 else kept + swap32(moved, lane)


def swap32(value, lane):
    odd = (lane & 32) != 0
    return jnp.where(odd, pltpu.roll(value, 32, 1), pltpu.roll(value, 96, 1))


def bins_kernel(place, recv_ref, cos_ref, sin_ref, out_ref, lines, low, high, real, turn, acc):
    lane = lax.broadcasted_iota(jnp.int32, (8, 128), 1)
    sub = lax.broadcasted_iota(jnp.int32, (8, 128), 0)
    upper = lane >= 64
    odd = (lane & 32) != 0

    acc[...] = jnp.zeros_like(acc)
    for f in range(4):
        for j in range(32):
            lines[j * 64 : j * 64 + 64, f * 128 : f * 128 + 128] = recv_ref[f * 32 + j, 0:64, :]
    tiles = []
    for tile in range(64):
        turned = tile >= 32
        source = 31 - (tile - 32) // 2 if turned else tile // 2
        pair = (tile % 2) * 2
        one = recv_ref[pair * 32 + source, 64:72, :].astype(jnp.float32)
        two = recv_ref[(pair + 1) * 32 + source, 64:72, :].astype(jnp.float32)
        shell = jnp.where(upper, pltpu.roll(two, 64, 1), one)
        mu = jnp.where(upper, two, pltpu.roll(one, 64, 1))
        tiles.append(shell + 256.0 * mu)
    rolled = [pltpu.roll(t, 1, 0) for t in tiles[32:]]
    moved = [pltpu.roll(t, 32, 1) for t in rolled]
    for m in range(32):
        first = jnp.where(lane < 32, moved[m - 1], moved[m])
        tiles[32 + m] = jnp.where(sub == 0, first, rolled[m])
    for tile in range(64):
        top = jnp.floor(tiles[tile] * (1.0 / 128.0))
        at = ((tile % 32) * 2 + tile // 32) * 8
        high[at : at + 8, :] = top
        low[at : at + 8, :] = tiles[tile] - 128.0 * top

    for part in range(HALF // TK):
        rows = slice(part * TK, part * TK + TK)
        real[rows, :] = jnp.dot(cos_ref[rows, :], lines[...], preferred_element_type=jnp.float32)
        turn[rows, :] = jnp.dot(sin_ref[rows, :], lines[...], preferred_element_type=jnp.float32)

    spot = place[1]
    col = (lane & 31).astype(jnp.float32)
    wave_x = (NZ // 4 + spot // 2).astype(jnp.float32)
    wave_y = (NZ // 8 + (spot % 2) * 128 + place[0] * 32).astype(jnp.float32) + col
    plane_square = wave_x * wave_x + wave_y * wave_y
    weight_one = jnp.where(odd, wave_y * wave_y, wave_x * wave_x) * 1.5
    mixed = wave_x * wave_y * 3.0
    linear = jnp.where(odd, wave_y, wave_x) * 3.0
    turn_sign = jnp.where(upper, -1.0, 1.0)
    step16 = lax.broadcasted_iota(jnp.int32, (16, 128), 0).astype(jnp.float32).astype(jnp.bfloat16)
    step128 = lax.broadcasted_iota(jnp.int32, (128, 128), 0).astype(jnp.float32).astype(jnp.bfloat16)

    def tile_body(m, carry):
        products = [[], []]
        for q in range(4):
            at = pl.multiple_of(m * 32 + q * 8, 8)
            k_row = at + sub
            first = k_row == 0
            wave_z = k_row.astype(jnp.float32)
            for sign in range(2):
                kz = wave_z if sign == 0 else jnp.where(first, -float(HALF), -wave_z)
                square = kz * kz
                inverse = 1.0 / (plane_square + square)
                weights = (
                    None,
                    weight_one * inverse,
                    jnp.where(odd, mixed, 1.5 * square) * inverse,
                    linear * kz * inverse,
                )
                spectra = []
                for f in range(4):
                    a = real[pl.ds(at, 8), f * 128 : f * 128 + 128]
                    b = pltpu.roll(turn[pl.ds(at, 8), f * 128 : f * 128 + 128], 64, 1) * turn_sign
                    if sign == 0:
                        spectra.append(a + jnp.where(first, 0.0, b))
                    else:
                        spectra.append(jnp.where(first, 0.0, a) - b)
                base = jnp.where(odd, pltpu.roll(spectra[0], 32, 1), spectra[0])
                cross = [base * s for s in spectra]
                products[sign].append([cross[0]] + [cross[f] * weights[f] for f in (1, 2, 3)])
        for sign in range(2):
            quad = products[sign]
            pairs = [
                (fold((quad[0][f], quad[2][f]), lane, 64), fold((quad[1][f], quad[3][f]), lane, 64))
                for f in range(4)
            ]
            even, other = pairs[0]
            tiles = [
                jnp.where(odd, pltpu.roll(other, 32, 1), even),
                jnp.where(odd, other, pltpu.roll(even, 96, 1)),
            ] + [fold(pairs[f], lane, 32) for f in (1, 2, 3)]
            at = pl.multiple_of(m * 16 + sign * 8, 8)
            lows = low[pl.ds(at, 8), :]
            highs = high[pl.ds(at, 8), :]
            total = None
            for r0 in range(0, 8, 4):
                vals, hots = [], []
                for r in range(r0, r0 + 4):
                    spread = jnp.broadcast_to(highs[r : r + 1], (16, 128)).astype(jnp.bfloat16)
                    hit = spread == step16
                    items = [jnp.broadcast_to(tiles[v][r : r + 1], (16, 128)).astype(jnp.bfloat16) for v in range(5)]
                    vals.append(jnp.concatenate(
                        [jnp.where(hit, item, jnp.bfloat16(0)) for item in items]
                        + [jnp.where(hit, jnp.bfloat16(1), jnp.bfloat16(0))], axis=0))
                    spread = jnp.broadcast_to(lows[r : r + 1], (16, 128)).astype(jnp.bfloat16)
                    hots.append(jnp.where(jnp.concatenate([spread] * 8, axis=0) == step128, jnp.bfloat16(1), jnp.bfloat16(0)))
                part = lax.dot_general(
                    jnp.concatenate(vals, axis=1), jnp.concatenate(hots, axis=1),
                    (((1,), (1,)), ((), ())), preferred_element_type=jnp.float32)
                total = part if total is None else total + part
            acc[...] += total
        return carry

    lax.fori_loop(0, HALF // 32, tile_body, 0, unroll=UNROLL)

    out_ref[0:32, :] = acc[0:32, :]
    out_ref[32:48, :] = acc[32:48, :] + acc[48:64, :] + acc[64:80, :] - 0.5 * acc[16:32, :]
    out_ref[48:64, :] = acc[80:96, :]


def bins(place, received, cos_table, sin_table):
    return pl.pallas_call(
        bins_kernel,
        in_specs=[pl.BlockSpec(memory_space=pltpu.SMEM)] + [pl.BlockSpec(memory_space=pltpu.VMEM)] * 3,
        out_specs=pl.BlockSpec(memory_space=pltpu.VMEM),
        scratch_shapes=[
            pltpu.VMEM((NZ, 512), jnp.bfloat16),
            pltpu.VMEM((512, 128), jnp.float32),
            pltpu.VMEM((512, 128), jnp.float32),
            pltpu.VMEM((HALF, 512), jnp.float32),
            pltpu.VMEM((HALF, 512), jnp.float32),
            pltpu.VMEM((96, 128), jnp.float32),
        ],
        out_shape=jax.ShapeDtypeStruct((64, 128), jnp.float32),
        compiler_params=pltpu.CompilerParams(vmem_limit_bytes=40 * 1024 * 1024),
        name="bins",
    )(place, received, cos_table, sin_table)


def total_over_devices(value):
    for bits in (1, 3, 9, 33, 7, 25, 97):
        value = value + lax.ppermute(value, BOTH, [(i, i ^ bits) for i in range(128)])
    return value


def body(fields, shells, mubins):
    field, spot = lax.axis_index("field"), lax.axis_index("gz")
    cos_table, sin_table = dft_tables()
    place = jnp.stack([field, spot, jnp.where(spot >= 16, 3 - field, field)]).astype(jnp.int32)
    sent = pack(place, fields, shells, mubins)
    received = lax.all_to_all(sent, BOTH, split_axis=0, concat_axis=0, tiled=True)
    partial = bins(place, received, jnp.asarray(cos_table), jnp.asarray(sin_table))
    total = total_over_devices(partial).reshape(4, MUBINS, SHELLS)
    return total[:3] / jnp.maximum(total[3], 1.0)[None]


def solution(mesh):
    in_specs = (P("gz", None, "field", None, None), P("gz", None, None), P("gz", None, None))
    return jax.shard_map(body, mesh=mesh, in_specs=in_specs, out_specs=P(), check_vma=False)
```

time: 108 us -> 89.9 us (0.83)
  Pallas kernels: 29.9 us -> 18.5 us
  local copies, waits for them, and re-layouts: 4.07 us -> 0.03 us
  waiting for transfers between devices: 25.2 us -> 23 us
  starting transfers between devices: 3.23 us -> 1.98 us
    pallas_call x2, Pallas kernels: 29.9 us -> 18.5 us  [the longest x1 13.7 us: bins(): pl.pallas_call(bins_kernel, in_specs=[pl.BlockSpec(memory_space=pltpu.SME...]
    unnamed x10 -> x4, local copies, waits for them, and re-layouts: 4.05 us -> 0.01 us
    ppermute x7, waiting for transfers between devices: 25.2 us -> 23 us  [total_over_devices(): lax.ppermute(value, BOTH, [(i, i ^ bits) for i in range(128)])]
    ppermute x7, starting transfers between devices: 3.23 us -> 1.98 us  [total_over_devices(): lax.ppermute(value, BOTH, [(i, i ^ bits) for i in range(128)])]
where the time goes in v2:
time: 89.9 us; the launch traced here: 88.7 us
  blocking collectives  44.4 us (49%)
  waiting for transfers between devices  23 us (26%)
  Pallas kernels  18.5 us (21%)
  starting transfers between devices  1.98 us (2%)
    all_to_all x1, blocking collectives, body(): lax.all_to_all(sent, BOTH, split_axis=0, concat_axis=0, tiled=True)  44.4 us
    ppermute x7, waiting for transfers between devices, total_over_devices(): lax.ppermute(value, BOTH, [(i, i ^ bits) for i in range(128)])  23 us
    pallas_call x1, Pallas kernels, bins(): pl.pallas_call(bins_kernel, in_specs=[pl.BlockSpec(memory_space=pltpu.SME...  13.7 us
    pallas_call x1, Pallas kernels, pack(): pl.pallas_call(pack_kernel, in_specs=[pl.BlockSpec(memory_space=pltpu.SME...  4.85 us
    ppermute x7, starting transfers between devices, total_over_devices(): lax.ppermute(value, BOTH, [(i, i ^ bits) for i in range(128)])  1.98 us
  transfers between devices with their start and end apart: 7, of which 7 were waited for; matrix products, arithmetic and copies ran while one was open for 0% of the time, Pallas kernels for 0%

profile of v2, /device:TPU:0, one launch (start us, length us, event | category | flops | bytes accessed | tf_op | source)
XLA Modules:
  0.0 88.7 jit_solution(452490658302961535)
XLA Ops:
  0.0 0.1 pad_add_fusion.place
  0.1 0.0 copy-start.1
  0.1 4.8 %pack.1 = bf16[128,72,128]{2,1,0:T(8,128)(2,1)S(1)} custom-call(s32[3]{0:T(128)S(1)} %pad_add_fusion.place, bf16[64,2,2,16,256]{4,3,2,1,0:T(8,128)(2,1)} %fields_hbm.1, s32[64,16,256]{2,1,0:T(8,128)} %shells_hbm.1, s32[64,16,256]{2,1,0:T(8,128)} %mubins_hbm.1), custom_call_target="tpu_custom_call" | custom-call | tf_op jit(solution)/shard_map/pack/pallas_call | solution.py:107
  4.9 0.0 copy-start
  4.9 44.4 %all_to_all.5.recv_ref = bf16[128,72,128]{2,1,0:T(8,128)(2,1)S(1)} all-to-all(bf16[128,72,128]{2,1,0:T(8,128)(2,1)S(1)} %pack.1), channel_id=1, replica_groups=mesh['field'=4,'gz'=32] {'field','gz'}, dimensions={0} | all-to-all | bytes 4718592 | tf_op jit(solution)/shard_map/all_to_all | solution.py:282
  49.3 0.0 copy-done.1
  49.3 0.0 copy-done
  49.3 13.7 %bins.1 = f32[64,128]{1,0:T(8,128)S(1)} custom-call(s32[3]{0:T(128)S(1)} %pad_add_fusion.place, bf16[128,72,128]{2,1,0:T(8,128)(2,1)S(1)} %all_to_all.5.recv_ref, bf16[1024,2048]{1,0:T(8,128)(2,1)S(1)} %copy-done.1, bf16[1024,2048]{1,0:T(8,128)(2,1)S(1)} %copy-done), custom_call_target="tpu_custom_call" | custom-call | tf_op jit(solution)/shard_map/bins/pallas_call | solution.py:253
  63.0 0.1 collective-permute-start
  63.1 1.2 %collective-permute-done = f32[64,128]{1,0:T(8,128)S(1)} collective-permute-done((f32[64,128]{1,0:T(8,128)S(1)}, f32[64,128]{1,0:T(8,128)S(1)}, u32[]{:S(2)}, u32[]{:S(2)}) %collective-permute-start) | collective-permute-done | bytes 32800 | tf_op jit(solution)/shard_map/ppermute | solution.py:273
  64.3 0.0 collective-permute-start.1
  64.3 3.3 %collective-permute-done.1 = f32[64,128]{1,0:T(8,128)S(1)} collective-permute-done((f32[64,128]{1,0:T(8,128)S(1)}, f32[64,128]{1,0:T(8,128)S(1)}, u32[]{:S(2)}, u32[]{:S(2)}) %collective-permute-start.1) | collective-permute-done | bytes 32800 | tf_op jit(solution)/shard_map/ppermute | solution.py:273
  67.6 0.2 collective-permute-start.2
  67.8 3.1 %collective-permute-done.2 = f32[64,128]{1,0:T(8,128)S(1)} collective-permute-done((f32[64,128]{1,0:T(8,128)S(1)}, f32[64,128]{1,0:T(8,128)S(1)}, u32[]{:S(2)}, u32[]{:S(2)}) %collective-permute-start.2) | collective-permute-done | bytes 32800 | tf_op jit(solution)/shard_map/ppermute | solution.py:273
  71.0 0.4 collective-permute-start.3
  71.3 3.0 %collective-permute-done.3 = f32[64,128]{1,0:T(8,128)S(1)} collective-permute-done((f32[64,128]{1,0:T(8,128)S(1)}, f32[64,128]{1,0:T(8,128)S(1)}, u32[]{:S(2)}, u32[]{:S(2)}) %collective-permute-start.3) | collective-permute-done | bytes 32800 | tf_op jit(solution)/shard_map/ppermute | solution.py:273
  74.3 0.0 collective-permute-start.4
  74.3 4.5 %collective-permute-done.4 = f32[64,128]{1,0:T(8,128)S(1)} collective-permute-done((f32[64,128]{1,0:T(8,128)S(1)}, f32[64,128]{1,0:T(8,128)S(1)}, u32[]{:S(2)}, u32[]{:S(2)}) %collective-permute-start.4) | collective-permute-done | bytes 32800 | tf_op jit(solution)/shard_map/ppermute | solution.py:273
  78.9 0.4 collective-permute-start.5
  79.3 4.1 %collective-permute-done.5 = f32[64,128]{1,0:T(8,128)S(1)} collective-permute-done((f32[64,128]{1,0:T(8,128)S(1)}, f32[64,128]{1,0:T(8,128)S(1)}, u32[]{:S(2)}, u32[]{:S(2)}) %collective-permute-start.5) | collective-permute-done | bytes 32800 | tf_op jit(solution)/shard_map/ppermute | solution.py:273
  83.5 0.9 %collective-permute-start.6 = (f32[64,128]{1,0:T(8,128)S(1)}, f32[64,128]{1,0:T(8,128)S(1)}, u32[]{:S(2)}, u32[]{:S(2)}) collective-permute-start(f32[64,128]{1,0:T(8,128)S(1)} %add.26), channel_id=1, source_target_pairs={{0,97},{1,96},{2,99},{3,98},{4,101},{5,100},{6,103},{7,102},{8,105... | collective-permute-start | bytes 98312 | tf_op jit(solution)/shard_map/ppermute | solution.py:273
  84.4 3.6 %collective-permute-done.6 = f32[64,128]{1,0:T(8,128)S(1)} collective-permute-done((f32[64,128]{1,0:T(8,128)S(1)}, f32[64,128]{1,0:T(8,128)S(1)}, u32[]{:S(2)}, u32[]{:S(2)}) %collective-permute-start.6) | collective-permute-done | bytes 32800 | tf_op jit(solution)/shard_map/ppermute | solution.py:273
  88.1 0.6 broadcast_divide_fusion
  (11 shorter events, 0.1 us)
Async XLA Ops:
  0.1 49.2 %copy-start.1 = (bf16[1024,2048]{1,0:T(8,128)(2,1)S(1)}, bf16[1024,2048]{1,0:T(8,128)(2,1)}, u32[]{:S(2)}) copy-start(bf16[1024,2048]{1,0:T(8,128)(2,1)} %constant.19.clone.cos_ref) | copy-start | bytes 12582916
  4.9 44.4 %copy-start = (bf16[1024,2048]{1,0:T(8,128)(2,1)S(1)}, bf16[1024,2048]{1,0:T(8,128)(2,1)}, u32[]{:S(2)}) copy-start(bf16[1024,2048]{1,0:T(8,128)(2,1)} %constant.20.clone.sin_ref) | copy-start | bytes 12582916
  63.0 1.3 %collective-permute-start = (f32[64,128]{1,0:T(8,128)S(1)}, f32[64,128]{1,0:T(8,128)S(1)}, u32[]{:S(2)}, u32[]{:S(2)}) collective-permute-start(f32[64,128]{1,0:T(8,128)S(1)} %bins.1), channel_id=1, source_target_pairs={{0,1},{1,0},{2,3},{3,2},{4,5},{5,4},{6,7},{7,6},{8,9},{9,8},{10,11... | collective-permute-start | bytes 98312 | tf_op jit(solution)/shard_map/ppermute | solution.py:273
  64.3 3.3 %collective-permute-start.1 = (f32[64,128]{1,0:T(8,128)S(1)}, f32[64,128]{1,0:T(8,128)S(1)}, u32[]{:S(2)}, u32[]{:S(2)}) collective-permute-start(f32[64,128]{1,0:T(8,128)S(1)} %add.21), channel_id=1, source_target_pairs={{0,3},{1,2},{2,1},{3,0},{4,7},{5,6},{6,5},{7,4},{8,11},{9,10},{10,... | collective-permute-start | bytes 98312 | tf_op jit(solution)/shard_map/ppermute | solution.py:273
  67.6 3.3 %collective-permute-start.2 = (f32[64,128]{1,0:T(8,128)S(1)}, f32[64,128]{1,0:T(8,128)S(1)}, u32[]{:S(2)}, u32[]{:S(2)}) collective-permute-start(f32[64,128]{1,0:T(8,128)S(1)} %add.22), channel_id=1, source_target_pairs={{0,9},{1,8},{2,11},{3,10},{4,13},{5,12},{6,15},{7,14},{8,1},{9,0},... | collective-permute-start | bytes 98312 | tf_op jit(solution)/shard_map/ppermute | solution.py:273
  71.0 3.3 %collective-permute-start.3 = (f32[64,128]{1,0:T(8,128)S(1)}, f32[64,128]{1,0:T(8,128)S(1)}, u32[]{:S(2)}, u32[]{:S(2)}) collective-permute-start(f32[64,128]{1,0:T(8,128)S(1)} %add.23), channel_id=1, source_target_pairs={{0,33},{1,32},{2,35},{3,34},{4,37},{5,36},{6,39},{7,38},{8,41},{9,... | collective-permute-start | bytes 98312 | tf_op jit(solution)/shard_map/ppermute | solution.py:273
  74.3 4.6 %collective-permute-start.4 = (f32[64,128]{1,0:T(8,128)S(1)}, f32[64,128]{1,0:T(8,128)S(1)}, u32[]{:S(2)}, u32[]{:S(2)}) collective-permute-start(f32[64,128]{1,0:T(8,128)S(1)} %add.24), channel_id=1, source_target_pairs={{0,7},{1,6},{2,5},{3,4},{4,3},{5,2},{6,1},{7,0},{8,15},{9,14},{10,... | collective-permute-start | bytes 98312 | tf_op jit(solution)/shard_map/ppermute | solution.py:273
  78.9 4.6 %collective-permute-start.5 = (f32[64,128]{1,0:T(8,128)S(1)}, f32[64,128]{1,0:T(8,128)S(1)}, u32[]{:S(2)}, u32[]{:S(2)}) collective-permute-start(f32[64,128]{1,0:T(8,128)S(1)} %add.25), channel_id=1, source_target_pairs={{0,25},{1,24},{2,27},{3,26},{4,29},{5,28},{6,31},{7,30},{8,17},{9,... | collective-permute-start | bytes 98312 | tf_op jit(solution)/shard_map/ppermute | solution.py:273
  83.5 4.6 %collective-permute-start.6 = (f32[64,128]{1,0:T(8,128)S(1)}, f32[64,128]{1,0:T(8,128)S(1)}, u32[]{:S(2)}, u32[]{:S(2)}) collective-permute-start(f32[64,128]{1,0:T(8,128)S(1)} %add.26), channel_id=1, source_target_pairs={{0,97},{1,96},{2,99},{3,98},{4,101},{5,100},{6,103},{7,102},{8,105... | collective-permute-start | bytes 98312 | tf_op jit(solution)/shard_map/ppermute | solution.py:273

commit v3 on v2

--- a/solution.py
+++ b/solution.py
@@ -17,7 +17,7 @@
 COLS = 32
 ROWS = 72
 TK = 256
-UNROLL = 8
+UNROLL = 16
 BOTH = ("field", "gz")
 
 
@@ -55,7 +55,7 @@
         pltpu.make_async_copy(source.at[pl.ds(spot, 16)], index_ref.at[n], index_sems.at[n])
         for n, source in enumerate((shells_hbm, mubins_hbm))
     ]
-    for copy in index_copies + copies:
+    for copy in copies + index_copies:
         copy.start()
     row = lax.broadcasted_iota(jnp.int32, (256, 256), 0)
     col = lax.broadcasted_iota(jnp.int32, (256, 256), 1)
@@ -64,24 +64,6 @@
     order = (col == inner * 16 + row // 16).astype(jnp.bfloat16)
     turned = jnp.where(place[1] >= 16, 15 - inner, inner)
     turned = (col == turned * 16 + row // 16).astype(jnp.bfloat16)
-
-    for copy in index_copies:
-        copy.wait()
-    maps = [
-        jnp.dot(
-            turned,
-            index_ref[n].reshape(256, YROWS).astype(jnp.bfloat16),
-            preferred_element_type=jnp.float32,
-        ).reshape(16, 2, 8, YROWS)
-        for n in range(2)
-    ]
-    groups = [item[:, h].reshape(128, YROWS) for item in maps for h in range(2)]
-    for half in range(2):
-        quarters = swap_groups([g[:, half * 128 : half * 128 + 128] for g in groups], lane[:128])
-        for q in range(4):
-            block = quarters[q].reshape(16, 8, 128)
-            for p in range(PLANES):
-                out_ref[q * 32 + p * 2 + half, 64:72, :] = block[p].astype(jnp.bfloat16)
 
     for part in range(4):
         copies[part].wait()
@@ -101,6 +83,24 @@
                 block = quarters[q].astype(jnp.bfloat16).reshape(16, 16, 128)
                 for p in range(PLANES):
                     out_ref[q * 32 + p * 2 + half, start : start + 16, :] = block[p]
+
+    for copy in index_copies:
+        copy.wait()
+    maps = [
+        jnp.dot(
+            turned,
+            index_ref[n].reshape(256, YROWS).astype(jnp.bfloat16),
+            preferred_element_type=jnp.float32,
+        ).reshape(16, 2, 8, YROWS)
+        for n in range(2)
+    ]
+    groups = [item[:, h].reshape(128, YROWS) for item in maps for h in range(2)]
+    for half in range(2):
+        quarters = swap_groups([g[:, half * 128 : half * 128 + 128] for g in groups], lane[:128])
+        for q in range(4):
+            block = quarters[q].reshape(16, 8, 128)
+            for p in range(PLANES):
+                out_ref[q * 32 + p * 2 + half, 64:72, :] = block[p].astype(jnp.bfloat16)
 
 
 def pack(place, fields, shells, mubins):
@@ -181,6 +181,13 @@
     step16 = lax.broadcasted_iota(jnp.int32, (16, 128), 0).astype(jnp.float32).astype(jnp.bfloat16)
     step128 = lax.broadcasted_iota(jnp.int32, (128, 128), 0).astype(jnp.float32).astype(jnp.bfloat16)
 
+    last_inverse = 1.0 / (plane_square + float(HALF) * HALF)
+    for f in range(4):
+        at = slice(f * 128, f * 128 + 128)
+        a, b = real[0:8, at], pltpu.roll(turn[0:8, at], 64, 1) * turn_sign
+        real[0:8, at] = jnp.where(sub == 0, 0.5 * (a - b), a)
+        turn[0:8, at] = pltpu.roll(jnp.where(sub == 0, 0.5 * (a + b), b) * turn_sign, 64, 1)
+
     def tile_body(m, carry):
         products = [[], []]
         for q in range(4):
@@ -188,10 +195,12 @@
             k_row = at + sub
             first = k_row == 0
             wave_z = k_row.astype(jnp.float32)
+            plain_square = wave_z * wave_z
+            plain_inverse = 1.0 / (plane_square + plain_square)
             for sign in range(2):
                 kz = wave_z if sign == 0 else jnp.where(first, -float(HALF), -wave_z)
-                square = kz * kz
-                inverse = 1.0 / (plane_square + square)
+                square = plain_square if sign == 0 else jnp.where(first, float(HALF) * HALF, plain_square)
+                inverse = plain_inverse if sign == 0 else jnp.where(first, last_inverse, plain_inverse)
                 weights = (
                     None,
                     weight_one * inverse,
@@ -202,10 +211,7 @@
                 for f in range(4):
                     a = real[pl.ds(at, 8), f * 128 : f * 128 + 128]
                     b = pltpu.roll(turn[pl.ds(at, 8), f * 128 : f * 128 + 128], 64, 1) * turn_sign
-                    if sign == 0:
-                        spectra.append(a + jnp.where(first, 0.0, b))
-                    else:
-                        spectra.append(jnp.where(first, 0.0, a) - b)
+                    spectra.append(a + b if sign == 0 else a - b)
                 base = jnp.where(odd, pltpu.roll(spectra[0], 32, 1), spectra[0])
                 cross = [base * s for s in spectra]
                 products[sign].append([cross[0]] + [cross[f] * weights[f] for f in (1, 2, 3)])

time: 89.9 us -> 88.7 us (0.987)
  Pallas kernels: 18.5 us -> 17.4 us
where the time goes in v3:
time: 88.7 us; the launch traced here: 87.6 us
  blocking collectives  44.4 us (50%)
  waiting for transfers between devices  23 us (26%)
  Pallas kernels  17.4 us (20%)
  starting transfers between devices  1.98 us (2%)
    all_to_all x1, blocking collectives, body(): lax.all_to_all(sent, BOTH, split_axis=0, concat_axis=0, tiled=True)  44.4 us
    ppermute x7, waiting for transfers between devices, total_over_devices(): lax.ppermute(value, BOTH, [(i, i ^ bits) for i in range(128)])  23 us
    pallas_call x1, Pallas kernels, bins(): pl.pallas_call(bins_kernel, in_specs=[pl.BlockSpec(memory_space=pltpu.SME...  13 us
    pallas_call x1, Pallas kernels, pack(): pl.pallas_call(pack_kernel, in_specs=[pl.BlockSpec(memory_space=pltpu.SME...  4.39 us
    ppermute x7, starting transfers between devices, total_over_devices(): lax.ppermute(value, BOTH, [(i, i ^ bits) for i in range(128)])  1.98 us
  transfers between devices with their start and end apart: 7, of which 7 were waited for; matrix products, arithmetic and copies ran while one was open for 0% of the time, Pallas kernels for 0%

profile of v3, /device:TPU:0, one launch (start us, length us, event | category | flops | bytes accessed | tf_op | source)
XLA Modules:
  0.0 87.6 jit_solution(15605998907564355427)
XLA Ops:
  0.0 0.1 pad_add_fusion.place
  0.1 0.0 copy-start.1
  0.1 4.4 %pack.1 = bf16[128,72,128]{2,1,0:T(8,128)(2,1)S(1)} custom-call(s32[3]{0:T(128)S(1)} %pad_add_fusion.place, bf16[64,2,2,16,256]{4,3,2,1,0:T(8,128)(2,1)} %fields_hbm.1, s32[64,16,256]{2,1,0:T(8,128)} %shells_hbm.1, s32[64,16,256]{2,1,0:T(8,128)} %mubins_hbm.1), custom_call_target="tpu_custom_call" | custom-call | tf_op jit(solution)/shard_map/pack/pallas_call | solution.py:107
  4.5 0.0 copy-start
  4.5 44.4 %all_to_all.5.recv_ref = bf16[128,72,128]{2,1,0:T(8,128)(2,1)S(1)} all-to-all(bf16[128,72,128]{2,1,0:T(8,128)(2,1)S(1)} %pack.1), channel_id=1, replica_groups=mesh['field'=4,'gz'=32] {'field','gz'}, dimensions={0} | all-to-all | bytes 4718592 | tf_op jit(solution)/shard_map/all_to_all | solution.py:288
  48.9 0.0 copy-done.1
  48.9 0.0 copy-done
  48.9 13.0 %bins.1 = f32[64,128]{1,0:T(8,128)S(1)} custom-call(s32[3]{0:T(128)S(1)} %pad_add_fusion.place, bf16[128,72,128]{2,1,0:T(8,128)(2,1)S(1)} %all_to_all.5.recv_ref, bf16[1024,2048]{1,0:T(8,128)(2,1)S(1)} %copy-done.1, bf16[1024,2048]{1,0:T(8,128)(2,1)S(1)} %copy-done), custom_call_target="tpu_custom_call" | custom-call | tf_op jit(solution)/shard_map/bins/pallas_call | solution.py:259
  61.9 0.1 collective-permute-start
  62.0 1.2 %collective-permute-done = f32[64,128]{1,0:T(8,128)S(1)} collective-permute-done((f32[64,128]{1,0:T(8,128)S(1)}, f32[64,128]{1,0:T(8,128)S(1)}, u32[]{:S(2)}, u32[]{:S(2)}) %collective-permute-start) | collective-permute-done | bytes 32800 | tf_op jit(solution)/shard_map/ppermute | solution.py:279
  63.2 0.0 collective-permute-start.1
  63.2 3.3 %collective-permute-done.1 = f32[64,128]{1,0:T(8,128)S(1)} collective-permute-done((f32[64,128]{1,0:T(8,128)S(1)}, f32[64,128]{1,0:T(8,128)S(1)}, u32[]{:S(2)}, u32[]{:S(2)}) %collective-permute-start.1) | collective-permute-done | bytes 32800 | tf_op jit(solution)/shard_map/ppermute | solution.py:279
  66.5 0.2 collective-permute-start.2
  66.7 3.1 %collective-permute-done.2 = f32[64,128]{1,0:T(8,128)S(1)} collective-permute-done((f32[64,128]{1,0:T(8,128)S(1)}, f32[64,128]{1,0:T(8,128)S(1)}, u32[]{:S(2)}, u32[]{:S(2)}) %collective-permute-start.2) | collective-permute-done | bytes 32800 | tf_op jit(solution)/shard_map/ppermute | solution.py:279
  69.9 0.4 collective-permute-start.3
  70.2 3.0 %collective-permute-done.3 = f32[64,128]{1,0:T(8,128)S(1)} collective-permute-done((f32[64,128]{1,0:T(8,128)S(1)}, f32[64,128]{1,0:T(8,128)S(1)}, u32[]{:S(2)}, u32[]{:S(2)}) %collective-permute-start.3) | collective-permute-done | bytes 32800 | tf_op jit(solution)/shard_map/ppermute | solution.py:279
  73.2 0.0 collective-permute-start.4
  73.2 4.5 %collective-permute-done.4 = f32[64,128]{1,0:T(8,128)S(1)} collective-permute-done((f32[64,128]{1,0:T(8,128)S(1)}, f32[64,128]{1,0:T(8,128)S(1)}, u32[]{:S(2)}, u32[]{:S(2)}) %collective-permute-start.4) | collective-permute-done | bytes 32800 | tf_op jit(solution)/shard_map/ppermute | solution.py:279
  77.8 0.4 collective-permute-start.5
  78.2 4.1 %collective-permute-done.5 = f32[64,128]{1,0:T(8,128)S(1)} collective-permute-done((f32[64,128]{1,0:T(8,128)S(1)}, f32[64,128]{1,0:T(8,128)S(1)}, u32[]{:S(2)}, u32[]{:S(2)}) %collective-permute-start.5) | collective-permute-done | bytes 32800 | tf_op jit(solution)/shard_map/ppermute | solution.py:279
  82.3 0.9 %collective-permute-start.6 = (f32[64,128]{1,0:T(8,128)S(1)}, f32[64,128]{1,0:T(8,128)S(1)}, u32[]{:S(2)}, u32[]{:S(2)}) collective-permute-start(f32[64,128]{1,0:T(8,128)S(1)} %add.26), channel_id=1, source_target_pairs={{0,97},{1,96},{2,99},{3,98},{4,101},{5,100},{6,103},{7,102},{8,105... | collective-permute-start | bytes 98312 | tf_op jit(solution)/shard_map/ppermute | solution.py:279
  83.3 3.6 %collective-permute-done.6 = f32[64,128]{1,0:T(8,128)S(1)} collective-permute-done((f32[64,128]{1,0:T(8,128)S(1)}, f32[64,128]{1,0:T(8,128)S(1)}, u32[]{:S(2)}, u32[]{:S(2)}) %collective-permute-start.6) | collective-permute-done | bytes 32800 | tf_op jit(solution)/shard_map/ppermute | solution.py:279
  86.9 0.6 broadcast_divide_fusion
  (11 shorter events, 0.1 us)
Async XLA Ops:
  0.1 48.8 %copy-start.1 = (bf16[1024,2048]{1,0:T(8,128)(2,1)S(1)}, bf16[1024,2048]{1,0:T(8,128)(2,1)}, u32[]{:S(2)}) copy-start(bf16[1024,2048]{1,0:T(8,128)(2,1)} %constant.19.clone.cos_ref) | copy-start | bytes 12582916
  4.5 44.4 %copy-start = (bf16[1024,2048]{1,0:T(8,128)(2,1)S(1)}, bf16[1024,2048]{1,0:T(8,128)(2,1)}, u32[]{:S(2)}) copy-start(bf16[1024,2048]{1,0:T(8,128)(2,1)} %constant.20.clone.sin_ref) | copy-start | bytes 12582916
  61.9 1.3 %collective-permute-start = (f32[64,128]{1,0:T(8,128)S(1)}, f32[64,128]{1,0:T(8,128)S(1)}, u32[]{:S(2)}, u32[]{:S(2)}) collective-permute-start(f32[64,128]{1,0:T(8,128)S(1)} %bins.1), channel_id=1, source_target_pairs={{0,1},{1,0},{2,3},{3,2},{4,5},{5,4},{6,7},{7,6},{8,9},{9,8},{10,11... | collective-permute-start | bytes 98312 | tf_op jit(solution)/shard_map/ppermute | solution.py:279
  63.2 3.3 %collective-permute-start.1 = (f32[64,128]{1,0:T(8,128)S(1)}, f32[64,128]{1,0:T(8,128)S(1)}, u32[]{:S(2)}, u32[]{:S(2)}) collective-permute-start(f32[64,128]{1,0:T(8,128)S(1)} %add.21), channel_id=1, source_target_pairs={{0,3},{1,2},{2,1},{3,0},{4,7},{5,6},{6,5},{7,4},{8,11},{9,10},{10,... | collective-permute-start | bytes 98312 | tf_op jit(solution)/shard_map/ppermute | solution.py:279
  66.5 3.3 %collective-permute-start.2 = (f32[64,128]{1,0:T(8,128)S(1)}, f32[64,128]{1,0:T(8,128)S(1)}, u32[]{:S(2)}, u32[]{:S(2)}) collective-permute-start(f32[64,128]{1,0:T(8,128)S(1)} %add.22), channel_id=1, source_target_pairs={{0,9},{1,8},{2,11},{3,10},{4,13},{5,12},{6,15},{7,14},{8,1},{9,0},... | collective-permute-start | bytes 98312 | tf_op jit(solution)/shard_map/ppermute | solution.py:279
  69.9 3.3 %collective-permute-start.3 = (f32[64,128]{1,0:T(8,128)S(1)}, f32[64,128]{1,0:T(8,128)S(1)}, u32[]{:S(2)}, u32[]{:S(2)}) collective-permute-start(f32[64,128]{1,0:T(8,128)S(1)} %add.23), channel_id=1, source_target_pairs={{0,33},{1,32},{2,35},{3,34},{4,37},{5,36},{6,39},{7,38},{8,41},{9,... | collective-permute-start | bytes 98312 | tf_op jit(solution)/shard_map/ppermute | solution.py:279
  73.2 4.6 %collective-permute-start.4 = (f32[64,128]{1,0:T(8,128)S(1)}, f32[64,128]{1,0:T(8,128)S(1)}, u32[]{:S(2)}, u32[]{:S(2)}) collective-permute-start(f32[64,128]{1,0:T(8,128)S(1)} %add.24), channel_id=1, source_target_pairs={{0,7},{1,6},{2,5},{3,4},{4,3},{5,2},{6,1},{7,0},{8,15},{9,14},{10,... | collective-permute-start | bytes 98312 | tf_op jit(solution)/shard_map/ppermute | solution.py:279
  77.8 4.6 %collective-permute-start.5 = (f32[64,128]{1,0:T(8,128)S(1)}, f32[64,128]{1,0:T(8,128)S(1)}, u32[]{:S(2)}, u32[]{:S(2)}) collective-permute-start(f32[64,128]{1,0:T(8,128)S(1)} %add.25), channel_id=1, source_target_pairs={{0,25},{1,24},{2,27},{3,26},{4,29},{5,28},{6,31},{7,30},{8,17},{9,... | collective-permute-start | bytes 98312 | tf_op jit(solution)/shard_map/ppermute | solution.py:279
  82.3 4.6 %collective-permute-start.6 = (f32[64,128]{1,0:T(8,128)S(1)}, f32[64,128]{1,0:T(8,128)S(1)}, u32[]{:S(2)}, u32[]{:S(2)}) collective-permute-start(f32[64,128]{1,0:T(8,128)S(1)} %add.26), channel_id=1, source_target_pairs={{0,97},{1,96},{2,99},{3,98},{4,101},{5,100},{6,103},{7,102},{8,105... | collective-permute-start | bytes 98312 | tf_op jit(solution)/shard_map/ppermute | solution.py:279

commit v4 on v3

--- a/solution.py
+++ b/solution.py
@@ -55,8 +55,9 @@
         pltpu.make_async_copy(source.at[pl.ds(spot, 16)], index_ref.at[n], index_sems.at[n])
         for n, source in enumerate((shells_hbm, mubins_hbm))
     ]
-    for copy in copies + index_copies:
-        copy.start()
+    queue = copies + index_copies
+    queue[0].start()
+    queue[1].start()
     row = lax.broadcasted_iota(jnp.int32, (256, 256), 0)
     col = lax.broadcasted_iota(jnp.int32, (256, 256), 1)
     lane = lax.broadcasted_iota(jnp.int32, (256, 128), 1)
@@ -67,6 +68,7 @@
 
     for part in range(4):
         copies[part].wait()
+        queue[part + 2].start()
         start = part * 16
         parts = [
             jnp.dot(

time: 88.7 us -> 89.3 us (level)
  no operation moved by 1% of the time
where the time goes in v4:
time: 89.3 us; the launch traced here: 88.1 us
  blocking collectives  44.4 us (50%)
  waiting for transfers between devices  23 us (26%)
  Pallas kernels  17.9 us (20%)
  starting transfers between devices  1.98 us (2%)
    all_to_all x1, blocking collectives, body(): lax.all_to_all(sent, BOTH, split_axis=0, concat_axis=0, tiled=True)  44.4 us
    ppermute x7, waiting for transfers between devices, total_over_devices(): lax.ppermute(value, BOTH, [(i, i ^ bits) for i in range(128)])  23 us
    pallas_call x1, Pallas kernels, bins(): pl.pallas_call(bins_kernel, in_specs=[pl.BlockSpec(memory_space=pltpu.SME...  13 us
    pallas_call x1, Pallas kernels, pack(): pl.pallas_call(pack_kernel, in_specs=[pl.BlockSpec(memory_space=pltpu.SME...  4.88 us
    ppermute x7, starting transfers between devices, total_over_devices(): lax.ppermute(value, BOTH, [(i, i ^ bits) for i in range(128)])  1.98 us
  transfers between devices with their start and end apart: 7, of which 7 were waited for; matrix products, arithmetic and copies ran while one was open for 0% of the time, Pallas kernels for 0%

profile of v4, /device:TPU:0, one launch (start us, length us, event | category | flops | bytes accessed | tf_op | source)
XLA Modules:
  0.0 88.1 jit_solution(5647961205348526527)
XLA Ops:
  0.0 0.1 pad_add_fusion.place
  0.1 0.0 copy-start.1
  0.1 4.9 %pack.1 = bf16[128,72,128]{2,1,0:T(8,128)(2,1)S(1)} custom-call(s32[3]{0:T(128)S(1)} %pad_add_fusion.place, bf16[64,2,2,16,256]{4,3,2,1,0:T(8,128)(2,1)} %fields_hbm.1, s32[64,16,256]{2,1,0:T(8,128)} %shells_hbm.1, s32[64,16,256]{2,1,0:T(8,128)} %mubins_hbm.1), custom_call_target="tpu_custom_call" | custom-call | tf_op jit(solution)/shard_map/pack/pallas_call | solution.py:109
  5.0 0.0 copy-start
  5.0 44.4 %all_to_all.5.recv_ref = bf16[128,72,128]{2,1,0:T(8,128)(2,1)S(1)} all-to-all(bf16[128,72,128]{2,1,0:T(8,128)(2,1)S(1)} %pack.1), channel_id=1, replica_groups=mesh['field'=4,'gz'=32] {'field','gz'}, dimensions={0} | all-to-all | bytes 4718592 | tf_op jit(solution)/shard_map/all_to_all | solution.py:290
  49.4 0.0 copy-done.1
  49.4 0.0 copy-done
  49.4 13.0 %bins.1 = f32[64,128]{1,0:T(8,128)S(1)} custom-call(s32[3]{0:T(128)S(1)} %pad_add_fusion.place, bf16[128,72,128]{2,1,0:T(8,128)(2,1)S(1)} %all_to_all.5.recv_ref, bf16[1024,2048]{1,0:T(8,128)(2,1)S(1)} %copy-done.1, bf16[1024,2048]{1,0:T(8,128)(2,1)S(1)} %copy-done), custom_call_target="tpu_custom_call" | custom-call | tf_op jit(solution)/shard_map/bins/pallas_call | solution.py:261
  62.4 0.1 collective-permute-start
  62.5 1.2 %collective-permute-done = f32[64,128]{1,0:T(8,128)S(1)} collective-permute-done((f32[64,128]{1,0:T(8,128)S(1)}, f32[64,128]{1,0:T(8,128)S(1)}, u32[]{:S(2)}, u32[]{:S(2)}) %collective-permute-start) | collective-permute-done | bytes 32800 | tf_op jit(solution)/shard_map/ppermute | solution.py:281
  63.7 0.0 collective-permute-start.1
  63.7 3.3 %collective-permute-done.1 = f32[64,128]{1,0:T(8,128)S(1)} collective-permute-done((f32[64,128]{1,0:T(8,128)S(1)}, f32[64,128]{1,0:T(8,128)S(1)}, u32[]{:S(2)}, u32[]{:S(2)}) %collective-permute-start.1) | collective-permute-done | bytes 32800 | tf_op jit(solution)/shard_map/ppermute | solution.py:281
  67.0 0.2 collective-permute-start.2
  67.2 3.1 %collective-permute-done.2 = f32[64,128]{1,0:T(8,128)S(1)} collective-permute-done((f32[64,128]{1,0:T(8,128)S(1)}, f32[64,128]{1,0:T(8,128)S(1)}, u32[]{:S(2)}, u32[]{:S(2)}) %collective-permute-start.2) | collective-permute-done | bytes 32800 | tf_op jit(solution)/shard_map/ppermute | solution.py:281
  70.4 0.4 collective-permute-start.3
  70.7 3.0 %collective-permute-done.3 = f32[64,128]{1,0:T(8,128)S(1)} collective-permute-done((f32[64,128]{1,0:T(8,128)S(1)}, f32[64,128]{1,0:T(8,128)S(1)}, u32[]{:S(2)}, u32[]{:S(2)}) %collective-permute-start.3) | collective-permute-done | bytes 32800 | tf_op jit(solution)/shard_map/ppermute | solution.py:281
  73.7 0.0 collective-permute-start.4
  73.7 4.5 %collective-permute-done.4 = f32[64,128]{1,0:T(8,128)S(1)} collective-permute-done((f32[64,128]{1,0:T(8,128)S(1)}, f32[64,128]{1,0:T(8,128)S(1)}, u32[]{:S(2)}, u32[]{:S(2)}) %collective-permute-start.4) | collective-permute-done | bytes 32800 | tf_op jit(solution)/shard_map/ppermute | solution.py:281
  78.3 0.4 collective-permute-start.5
  78.7 4.1 %collective-permute-done.5 = f32[64,128]{1,0:T(8,128)S(1)} collective-permute-done((f32[64,128]{1,0:T(8,128)S(1)}, f32[64,128]{1,0:T(8,128)S(1)}, u32[]{:S(2)}, u32[]{:S(2)}) %collective-permute-start.5) | collective-permute-done | bytes 32800 | tf_op jit(solution)/shard_map/ppermute | solution.py:281
  82.8 0.9 %collective-permute-start.6 = (f32[64,128]{1,0:T(8,128)S(1)}, f32[64,128]{1,0:T(8,128)S(1)}, u32[]{:S(2)}, u32[]{:S(2)}) collective-permute-start(f32[64,128]{1,0:T(8,128)S(1)} %add.26), channel_id=1, source_target_pairs={{0,97},{1,96},{2,99},{3,98},{4,101},{5,100},{6,103},{7,102},{8,105... | collective-permute-start | bytes 98312 | tf_op jit(solution)/shard_map/ppermute | solution.py:281
  83.8 3.6 %collective-permute-done.6 = f32[64,128]{1,0:T(8,128)S(1)} collective-permute-done((f32[64,128]{1,0:T(8,128)S(1)}, f32[64,128]{1,0:T(8,128)S(1)}, u32[]{:S(2)}, u32[]{:S(2)}) %collective-permute-start.6) | collective-permute-done | bytes 32800 | tf_op jit(solution)/shard_map/ppermute | solution.py:281
  87.4 0.6 broadcast_divide_fusion
  (11 shorter events, 0.1 us)
Async XLA Ops:
  0.1 49.3 %copy-start.1 = (bf16[1024,2048]{1,0:T(8,128)(2,1)S(1)}, bf16[1024,2048]{1,0:T(8,128)(2,1)}, u32[]{:S(2)}) copy-start(bf16[1024,2048]{1,0:T(8,128)(2,1)} %constant.19.clone.cos_ref) | copy-start | bytes 12582916
  5.0 44.4 %copy-start = (bf16[1024,2048]{1,0:T(8,128)(2,1)S(1)}, bf16[1024,2048]{1,0:T(8,128)(2,1)}, u32[]{:S(2)}) copy-start(bf16[1024,2048]{1,0:T(8,128)(2,1)} %constant.20.clone.sin_ref) | copy-start | bytes 12582916
  62.4 1.3 %collective-permute-start = (f32[64,128]{1,0:T(8,128)S(1)}, f32[64,128]{1,0:T(8,128)S(1)}, u32[]{:S(2)}, u32[]{:S(2)}) collective-permute-start(f32[64,128]{1,0:T(8,128)S(1)} %bins.1), channel_id=1, source_target_pairs={{0,1},{1,0},{2,3},{3,2},{4,5},{5,4},{6,7},{7,6},{8,9},{9,8},{10,11... | collective-permute-start | bytes 98312 | tf_op jit(solution)/shard_map/ppermute | solution.py:281
  63.7 3.3 %collective-permute-start.1 = (f32[64,128]{1,0:T(8,128)S(1)}, f32[64,128]{1,0:T(8,128)S(1)}, u32[]{:S(2)}, u32[]{:S(2)}) collective-permute-start(f32[64,128]{1,0:T(8,128)S(1)} %add.21), channel_id=1, source_target_pairs={{0,3},{1,2},{2,1},{3,0},{4,7},{5,6},{6,5},{7,4},{8,11},{9,10},{10,... | collective-permute-start | bytes 98312 | tf_op jit(solution)/shard_map/ppermute | solution.py:281
  67.0 3.3 %collective-permute-start.2 = (f32[64,128]{1,0:T(8,128)S(1)}, f32[64,128]{1,0:T(8,128)S(1)}, u32[]{:S(2)}, u32[]{:S(2)}) collective-permute-start(f32[64,128]{1,0:T(8,128)S(1)} %add.22), channel_id=1, source_target_pairs={{0,9},{1,8},{2,11},{3,10},{4,13},{5,12},{6,15},{7,14},{8,1},{9,0},... | collective-permute-start | bytes 98312 | tf_op jit(solution)/shard_map/ppermute | solution.py:281
  70.4 3.3 %collective-permute-start.3 = (f32[64,128]{1,0:T(8,128)S(1)}, f32[64,128]{1,0:T(8,128)S(1)}, u32[]{:S(2)}, u32[]{:S(2)}) collective-permute-start(f32[64,128]{1,0:T(8,128)S(1)} %add.23), channel_id=1, source_target_pairs={{0,33},{1,32},{2,35},{3,34},{4,37},{5,36},{6,39},{7,38},{8,41},{9,... | collective-permute-start | bytes 98312 | tf_op jit(solution)/shard_map/ppermute | solution.py:281
  73.7 4.6 %collective-permute-start.4 = (f32[64,128]{1,0:T(8,128)S(1)}, f32[64,128]{1,0:T(8,128)S(1)}, u32[]{:S(2)}, u32[]{:S(2)}) collective-permute-start(f32[64,128]{1,0:T(8,128)S(1)} %add.24), channel_id=1, source_target_pairs={{0,7},{1,6},{2,5},{3,4},{4,3},{5,2},{6,1},{7,0},{8,15},{9,14},{10,... | collective-permute-start | bytes 98312 | tf_op jit(solution)/shard_map/ppermute | solution.py:281
  78.3 4.6 %collective-permute-start.5 = (f32[64,128]{1,0:T(8,128)S(1)}, f32[64,128]{1,0:T(8,128)S(1)}, u32[]{:S(2)}, u32[]{:S(2)}) collective-permute-start(f32[64,128]{1,0:T(8,128)S(1)} %add.25), channel_id=1, source_target_pairs={{0,25},{1,24},{2,27},{3,26},{4,29},{5,28},{6,31},{7,30},{8,17},{9,... | collective-permute-start | bytes 98312 | tf_op jit(solution)/shard_map/ppermute | solution.py:281
  82.8 4.6 %collective-permute-start.6 = (f32[64,128]{1,0:T(8,128)S(1)}, f32[64,128]{1,0:T(8,128)S(1)}, u32[]{:S(2)}, u32[]{:S(2)}) collective-permute-start(f32[64,128]{1,0:T(8,128)S(1)} %add.26), channel_id=1, source_target_pairs={{0,97},{1,96},{2,99},{3,98},{4,101},{5,100},{6,103},{7,102},{8,105... | collective-permute-start | bytes 98312 | tf_op jit(solution)/shard_map/ppermute | solution.py:281

commit v5 on v3

--- a/solution.py
+++ b/solution.py
@@ -66,7 +66,11 @@
     turned = (col == turned * 16 + row // 16).astype(jnp.bfloat16)
 
     for part in range(4):
-        copies[part].wait()
+        if part == 0:
+            copies[0].wait()
+        if part == 1:
+            for copy in copies[1:] + index_copies:
+                copy.wait()
         start = part * 16
         parts = [
             jnp.dot(
@@ -84,8 +88,6 @@
                 for p in range(PLANES):
                     out_ref[q * 32 + p * 2 + half, start : start + 16, :] = block[p]
 
-    for copy in index_copies:
-        copy.wait()
     maps = [
         jnp.dot(
             turned,

time: 88.7 us -> 88.4 us (level)
  no operation moved by 1% of the time
where the time goes in v5:
time: 88.4 us; the launch traced here: 87.2 us
  blocking collectives  44.4 us (50%)
  waiting for transfers between devices  23 us (26%)
  Pallas kernels  17 us (19%)
  starting transfers between devices  1.98 us (2%)
    all_to_all x1, blocking collectives, body(): lax.all_to_all(sent, BOTH, split_axis=0, concat_axis=0, tiled=True)  44.4 us
    ppermute x7, waiting for transfers between devices, total_over_devices(): lax.ppermute(value, BOTH, [(i, i ^ bits) for i in range(128)])  23 us
    pallas_call x1, Pallas kernels, bins(): pl.pallas_call(bins_kernel, in_specs=[pl.BlockSpec(memory_space=pltpu.SME...  13 us
    pallas_call x1, Pallas kernels, pack(): pl.pallas_call(pack_kernel, in_specs=[pl.BlockSpec(memory_space=pltpu.SME...  4 us
    ppermute x7, starting transfers between devices, total_over_devices(): lax.ppermute(value, BOTH, [(i, i ^ bits) for i in range(128)])  1.98 us
  transfers between devices with their start and end apart: 7, of which 7 were waited for; matrix products, arithmetic and copies ran while one was open for 0% of the time, Pallas kernels for 0%

profile of v5, /device:TPU:0, one launch (start us, length us, event | category | flops | bytes accessed | tf_op | source)
XLA Modules:
  0.0 87.2 jit_solution(10906421376784889691)
XLA Ops:
  0.0 0.1 pad_add_fusion.place
  0.1 0.0 copy-start.1
  0.1 4.0 %pack.1 = bf16[128,72,128]{2,1,0:T(8,128)(2,1)S(1)} custom-call(s32[3]{0:T(128)S(1)} %pad_add_fusion.place, bf16[64,2,2,16,256]{4,3,2,1,0:T(8,128)(2,1)} %fields_hbm.1, s32[64,16,256]{2,1,0:T(8,128)} %shells_hbm.1, s32[64,16,256]{2,1,0:T(8,128)} %mubins_hbm.1), custom_call_target="tpu_custom_call" | custom-call | tf_op jit(solution)/shard_map/pack/pallas_call | solution.py:109
  4.1 0.0 copy-start
  4.1 44.4 %all_to_all.5.recv_ref = bf16[128,72,128]{2,1,0:T(8,128)(2,1)S(1)} all-to-all(bf16[128,72,128]{2,1,0:T(8,128)(2,1)S(1)} %pack.1), channel_id=1, replica_groups=mesh['field'=4,'gz'=32] {'field','gz'}, dimensions={0} | all-to-all | bytes 4718592 | tf_op jit(solution)/shard_map/all_to_all | solution.py:290
  48.5 0.0 copy-done.1
  48.5 0.0 copy-done
  48.5 13.0 %bins.1 = f32[64,128]{1,0:T(8,128)S(1)} custom-call(s32[3]{0:T(128)S(1)} %pad_add_fusion.place, bf16[128,72,128]{2,1,0:T(8,128)(2,1)S(1)} %all_to_all.5.recv_ref, bf16[1024,2048]{1,0:T(8,128)(2,1)S(1)} %copy-done.1, bf16[1024,2048]{1,0:T(8,128)(2,1)S(1)} %copy-done), custom_call_target="tpu_custom_call" | custom-call | tf_op jit(solution)/shard_map/bins/pallas_call | solution.py:261
  61.5 0.1 collective-permute-start
  61.6 1.2 %collective-permute-done = f32[64,128]{1,0:T(8,128)S(1)} collective-permute-done((f32[64,128]{1,0:T(8,128)S(1)}, f32[64,128]{1,0:T(8,128)S(1)}, u32[]{:S(2)}, u32[]{:S(2)}) %collective-permute-start) | collective-permute-done | bytes 32800 | tf_op jit(solution)/shard_map/ppermute | solution.py:281
  62.8 0.0 collective-permute-start.1
  62.8 3.3 %collective-permute-done.1 = f32[64,128]{1,0:T(8,128)S(1)} collective-permute-done((f32[64,128]{1,0:T(8,128)S(1)}, f32[64,128]{1,0:T(8,128)S(1)}, u32[]{:S(2)}, u32[]{:S(2)}) %collective-permute-start.1) | collective-permute-done | bytes 32800 | tf_op jit(solution)/shard_map/ppermute | solution.py:281
  66.2 0.2 collective-permute-start.2
  66.4 3.1 %collective-permute-done.2 = f32[64,128]{1,0:T(8,128)S(1)} collective-permute-done((f32[64,128]{1,0:T(8,128)S(1)}, f32[64,128]{1,0:T(8,128)S(1)}, u32[]{:S(2)}, u32[]{:S(2)}) %collective-permute-start.2) | collective-permute-done | bytes 32800 | tf_op jit(solution)/shard_map/ppermute | solution.py:281
  69.5 0.4 collective-permute-start.3
  69.9 3.0 %collective-permute-done.3 = f32[64,128]{1,0:T(8,128)S(1)} collective-permute-done((f32[64,128]{1,0:T(8,128)S(1)}, f32[64,128]{1,0:T(8,128)S(1)}, u32[]{:S(2)}, u32[]{:S(2)}) %collective-permute-start.3) | collective-permute-done | bytes 32800 | tf_op jit(solution)/shard_map/ppermute | solution.py:281
  72.8 0.0 collective-permute-start.4
  72.9 4.5 %collective-permute-done.4 = f32[64,128]{1,0:T(8,128)S(1)} collective-permute-done((f32[64,128]{1,0:T(8,128)S(1)}, f32[64,128]{1,0:T(8,128)S(1)}, u32[]{:S(2)}, u32[]{:S(2)}) %collective-permute-start.4) | collective-permute-done | bytes 32800 | tf_op jit(solution)/shard_map/ppermute | solution.py:281
  77.4 0.4 collective-permute-start.5
  77.8 4.1 %collective-permute-done.5 = f32[64,128]{1,0:T(8,128)S(1)} collective-permute-done((f32[64,128]{1,0:T(8,128)S(1)}, f32[64,128]{1,0:T(8,128)S(1)}, u32[]{:S(2)}, u32[]{:S(2)}) %collective-permute-start.5) | collective-permute-done | bytes 32800 | tf_op jit(solution)/shard_map/ppermute | solution.py:281
  82.0 0.9 %collective-permute-start.6 = (f32[64,128]{1,0:T(8,128)S(1)}, f32[64,128]{1,0:T(8,128)S(1)}, u32[]{:S(2)}, u32[]{:S(2)}) collective-permute-start(f32[64,128]{1,0:T(8,128)S(1)} %add.26), channel_id=1, source_target_pairs={{0,97},{1,96},{2,99},{3,98},{4,101},{5,100},{6,103},{7,102},{8,105... | collective-permute-start | bytes 98312 | tf_op jit(solution)/shard_map/ppermute | solution.py:281
  82.9 3.6 %collective-permute-done.6 = f32[64,128]{1,0:T(8,128)S(1)} collective-permute-done((f32[64,128]{1,0:T(8,128)S(1)}, f32[64,128]{1,0:T(8,128)S(1)}, u32[]{:S(2)}, u32[]{:S(2)}) %collective-permute-start.6) | collective-permute-done | bytes 32800 | tf_op jit(solution)/shard_map/ppermute | solution.py:281
  86.6 0.6 broadcast_divide_fusion
  (11 shorter events, 0.1 us)
Async XLA Ops:
  0.1 48.4 %copy-start.1 = (bf16[1024,2048]{1,0:T(8,128)(2,1)S(1)}, bf16[1024,2048]{1,0:T(8,128)(2,1)}, u32[]{:S(2)}) copy-start(bf16[1024,2048]{1,0:T(8,128)(2,1)} %constant.19.clone.cos_ref) | copy-start | bytes 12582916
  4.1 44.4 %copy-start = (bf16[1024,2048]{1,0:T(8,128)(2,1)S(1)}, bf16[1024,2048]{1,0:T(8,128)(2,1)}, u32[]{:S(2)}) copy-start(bf16[1024,2048]{1,0:T(8,128)(2,1)} %constant.20.clone.sin_ref) | copy-start | bytes 12582916
  61.5 1.3 %collective-permute-start = (f32[64,128]{1,0:T(8,128)S(1)}, f32[64,128]{1,0:T(8,128)S(1)}, u32[]{:S(2)}, u32[]{:S(2)}) collective-permute-start(f32[64,128]{1,0:T(8,128)S(1)} %bins.1), channel_id=1, source_target_pairs={{0,1},{1,0},{2,3},{3,2},{4,5},{5,4},{6,7},{7,6},{8,9},{9,8},{10,11... | collective-permute-start | bytes 98312 | tf_op jit(solution)/shard_map/ppermute | solution.py:281
  62.8 3.3 %collective-permute-start.1 = (f32[64,128]{1,0:T(8,128)S(1)}, f32[64,128]{1,0:T(8,128)S(1)}, u32[]{:S(2)}, u32[]{:S(2)}) collective-permute-start(f32[64,128]{1,0:T(8,128)S(1)} %add.21), channel_id=1, source_target_pairs={{0,3},{1,2},{2,1},{3,0},{4,7},{5,6},{6,5},{7,4},{8,11},{9,10},{10,... | collective-permute-start | bytes 98312 | tf_op jit(solution)/shard_map/ppermute | solution.py:281
  66.2 3.3 %collective-permute-start.2 = (f32[64,128]{1,0:T(8,128)S(1)}, f32[64,128]{1,0:T(8,128)S(1)}, u32[]{:S(2)}, u32[]{:S(2)}) collective-permute-start(f32[64,128]{1,0:T(8,128)S(1)} %add.22), channel_id=1, source_target_pairs={{0,9},{1,8},{2,11},{3,10},{4,13},{5,12},{6,15},{7,14},{8,1},{9,0},... | collective-permute-start | bytes 98312 | tf_op jit(solution)/shard_map/ppermute | solution.py:281
  69.5 3.3 %collective-permute-start.3 = (f32[64,128]{1,0:T(8,128)S(1)}, f32[64,128]{1,0:T(8,128)S(1)}, u32[]{:S(2)}, u32[]{:S(2)}) collective-permute-start(f32[64,128]{1,0:T(8,128)S(1)} %add.23), channel_id=1, source_target_pairs={{0,33},{1,32},{2,35},{3,34},{4,37},{5,36},{6,39},{7,38},{8,41},{9,... | collective-permute-start | bytes 98312 | tf_op jit(solution)/shard_map/ppermute | solution.py:281
  72.8 4.6 %collective-permute-start.4 = (f32[64,128]{1,0:T(8,128)S(1)}, f32[64,128]{1,0:T(8,128)S(1)}, u32[]{:S(2)}, u32[]{:S(2)}) collective-permute-start(f32[64,128]{1,0:T(8,128)S(1)} %add.24), channel_id=1, source_target_pairs={{0,7},{1,6},{2,5},{3,4},{4,3},{5,2},{6,1},{7,0},{8,15},{9,14},{10,... | collective-permute-start | bytes 98312 | tf_op jit(solution)/shard_map/ppermute | solution.py:281
  77.4 4.6 %collective-permute-start.5 = (f32[64,128]{1,0:T(8,128)S(1)}, f32[64,128]{1,0:T(8,128)S(1)}, u32[]{:S(2)}, u32[]{:S(2)}) collective-permute-start(f32[64,128]{1,0:T(8,128)S(1)} %add.25), channel_id=1, source_target_pairs={{0,25},{1,24},{2,27},{3,26},{4,29},{5,28},{6,31},{7,30},{8,17},{9,... | collective-permute-start | bytes 98312 | tf_op jit(solution)/shard_map/ppermute | solution.py:281
  82.0 4.6 %collective-permute-start.6 = (f32[64,128]{1,0:T(8,128)S(1)}, f32[64,128]{1,0:T(8,128)S(1)}, u32[]{:S(2)}, u32[]{:S(2)}) collective-permute-start(f32[64,128]{1,0:T(8,128)S(1)} %add.26), channel_id=1, source_target_pairs={{0,97},{1,96},{2,99},{3,98},{4,101},{5,100},{6,103},{7,102},{8,105... | collective-permute-start | bytes 98312 | tf_op jit(solution)/shard_map/ppermute | solution.py:281

commit v6 on v2

--- a/solution.py
+++ b/solution.py
@@ -17,7 +17,7 @@
 COLS = 32
 ROWS = 72
 TK = 256
-UNROLL = 8
+UNROLL = 16
 BOTH = ("field", "gz")
 
 
@@ -65,7 +65,7 @@
     turned = jnp.where(place[1] >= 16, 15 - inner, inner)
     turned = (col == turned * 16 + row // 16).astype(jnp.bfloat16)
 
-    for copy in index_copies:
+    for copy in index_copies + copies[:1]:
         copy.wait()
     maps = [
         jnp.dot(
@@ -84,7 +84,9 @@
                 out_ref[q * 32 + p * 2 + half, 64:72, :] = block[p].astype(jnp.bfloat16)
 
     for part in range(4):
-        copies[part].wait()
+        if part == 1:
+            for copy in copies[1:]:
+                copy.wait()
         start = part * 16
         parts = [
             jnp.dot(
@@ -181,6 +183,13 @@
     step16 = lax.broadcasted_iota(jnp.int32, (16, 128), 0).astype(jnp.float32).astype(jnp.bfloat16)
     step128 = lax.broadcasted_iota(jnp.int32, (128, 128), 0).astype(jnp.float32).astype(jnp.bfloat16)
 
+    last_inverse = 1.0 / (plane_square + float(HALF) * HALF)
+    for f in range(4):
+        at = slice(f * 128, f * 128 + 128)
+        a, b = real[0:8, at], pltpu.roll(turn[0:8, at], 64, 1) * turn_sign
+        real[0:8, at] = jnp.where(sub == 0, 0.5 * (a - b), a)
+        turn[0:8, at] = pltpu.roll(jnp.where(sub == 0, 0.5 * (a + b), b) * turn_sign, 64, 1)
+
     def tile_body(m, carry):
         products = [[], []]
         for q in range(4):
@@ -188,10 +197,12 @@
             k_row = at + sub
             first = k_row == 0
             wave_z = k_row.astype(jnp.float32)
+            plain_square = wave_z * wave_z
+            plain_inverse = 1.0 / (plane_square + plain_square)
             for sign in range(2):
                 kz = wave_z if sign == 0 else jnp.where(first, -float(HALF), -wave_z)
-                square = kz * kz
-                inverse = 1.0 / (plane_square + square)
+                square = plain_square if sign == 0 else jnp.where(first, float(HALF) * HALF, plain_square)
+                inverse = plain_inverse if sign == 0 else jnp.where(first, last_inverse, plain_inverse)
                 weights = (
                     None,
                     weight_one * inverse,
@@ -202,10 +213,7 @@
                 for f in range(4):
                     a = real[pl.ds(at, 8), f * 128 : f * 128 + 128]
                     b = pltpu.roll(turn[pl.ds(at, 8), f * 128 : f * 128 + 128], 64, 1) * turn_sign
-                    if sign == 0:
-                        spectra.append(a + jnp.where(first, 0.0, b))
-                    else:
-                        spectra.append(jnp.where(first, 0.0, a) - b)
+                    spectra.append(a + b if sign == 0 else a - b)
                 base = jnp.where(odd, pltpu.roll(spectra[0], 32, 1), spectra[0])
                 cross = [base * s for s in spectra]
                 products[sign].append([cross[0]] + [cross[f] * weights[f] for f in (1, 2, 3)])

time: 89.9 us -> 88.6 us (0.986)
  Pallas kernels: 18.5 us -> 17.3 us
where the time goes in v6:
time: 88.6 us; the launch traced here: 87.4 us
  blocking collectives  44.4 us (50%)
  waiting for transfers between devices  23 us (26%)
  Pallas kernels  17.3 us (20%)
  starting transfers between devices  1.98 us (2%)
    all_to_all x1, blocking collectives, body(): lax.all_to_all(sent, BOTH, split_axis=0, concat_axis=0, tiled=True)  44.4 us
    ppermute x7, waiting for transfers between devices, total_over_devices(): lax.ppermute(value, BOTH, [(i, i ^ bits) for i in range(128)])  23 us
    pallas_call x1, Pallas kernels, bins(): pl.pallas_call(bins_kernel, in_specs=[pl.BlockSpec(memory_space=pltpu.SME...  13 us
    pallas_call x1, Pallas kernels, pack(): pl.pallas_call(pack_kernel, in_specs=[pl.BlockSpec(memory_space=pltpu.SME...  4.26 us
    ppermute x7, starting transfers between devices, total_over_devices(): lax.ppermute(value, BOTH, [(i, i ^ bits) for i in range(128)])  1.98 us
  transfers between devices with their start and end apart: 7, of which 7 were waited for; matrix products, arithmetic and copies ran while one was open for 0% of the time, Pallas kernels for 0%

profile of v6, /device:TPU:0, one launch (start us, length us, event | category | flops | bytes accessed | tf_op | source)
XLA Modules:
  0.0 87.4 jit_solution(1788533186194418995)
XLA Ops:
  0.0 0.1 pad_add_fusion.place
  0.1 0.0 copy-start.1
  0.1 4.3 %pack.1 = bf16[128,72,128]{2,1,0:T(8,128)(2,1)S(1)} custom-call(s32[3]{0:T(128)S(1)} %pad_add_fusion.place, bf16[64,2,2,16,256]{4,3,2,1,0:T(8,128)(2,1)} %fields_hbm.1, s32[64,16,256]{2,1,0:T(8,128)} %shells_hbm.1, s32[64,16,256]{2,1,0:T(8,128)} %mubins_hbm.1), custom_call_target="tpu_custom_call" | custom-call | tf_op jit(solution)/shard_map/pack/pallas_call | solution.py:109
  4.3 0.0 copy-start
  4.4 44.4 %all_to_all.5.recv_ref = bf16[128,72,128]{2,1,0:T(8,128)(2,1)S(1)} all-to-all(bf16[128,72,128]{2,1,0:T(8,128)(2,1)S(1)} %pack.1), channel_id=1, replica_groups=mesh['field'=4,'gz'=32] {'field','gz'}, dimensions={0} | all-to-all | bytes 4718592 | tf_op jit(solution)/shard_map/all_to_all | solution.py:290
  48.7 0.0 copy-done.1
  48.7 0.0 copy-done
  48.7 13.0 %bins.1 = f32[64,128]{1,0:T(8,128)S(1)} custom-call(s32[3]{0:T(128)S(1)} %pad_add_fusion.place, bf16[128,72,128]{2,1,0:T(8,128)(2,1)S(1)} %all_to_all.5.recv_ref, bf16[1024,2048]{1,0:T(8,128)(2,1)S(1)} %copy-done.1, bf16[1024,2048]{1,0:T(8,128)(2,1)S(1)} %copy-done), custom_call_target="tpu_custom_call" | custom-call | tf_op jit(solution)/shard_map/bins/pallas_call | solution.py:261
  61.8 0.1 collective-permute-start
  61.9 1.2 %collective-permute-done = f32[64,128]{1,0:T(8,128)S(1)} collective-permute-done((f32[64,128]{1,0:T(8,128)S(1)}, f32[64,128]{1,0:T(8,128)S(1)}, u32[]{:S(2)}, u32[]{:S(2)}) %collective-permute-start) | collective-permute-done | bytes 32800 | tf_op jit(solution)/shard_map/ppermute | solution.py:281
  63.1 0.0 collective-permute-start.1
  63.1 3.3 %collective-permute-done.1 = f32[64,128]{1,0:T(8,128)S(1)} collective-permute-done((f32[64,128]{1,0:T(8,128)S(1)}, f32[64,128]{1,0:T(8,128)S(1)}, u32[]{:S(2)}, u32[]{:S(2)}) %collective-permute-start.1) | collective-permute-done | bytes 32800 | tf_op jit(solution)/shard_map/ppermute | solution.py:281
  66.4 0.2 collective-permute-start.2
  66.6 3.1 %collective-permute-done.2 = f32[64,128]{1,0:T(8,128)S(1)} collective-permute-done((f32[64,128]{1,0:T(8,128)S(1)}, f32[64,128]{1,0:T(8,128)S(1)}, u32[]{:S(2)}, u32[]{:S(2)}) %collective-permute-start.2) | collective-permute-done | bytes 32800 | tf_op jit(solution)/shard_map/ppermute | solution.py:281
  69.8 0.4 collective-permute-start.3
  70.1 3.0 %collective-permute-done.3 = f32[64,128]{1,0:T(8,128)S(1)} collective-permute-done((f32[64,128]{1,0:T(8,128)S(1)}, f32[64,128]{1,0:T(8,128)S(1)}, u32[]{:S(2)}, u32[]{:S(2)}) %collective-permute-start.3) | collective-permute-done | bytes 32800 | tf_op jit(solution)/shard_map/ppermute | solution.py:281
  73.1 0.0 collective-permute-start.4
  73.1 4.5 %collective-permute-done.4 = f32[64,128]{1,0:T(8,128)S(1)} collective-permute-done((f32[64,128]{1,0:T(8,128)S(1)}, f32[64,128]{1,0:T(8,128)S(1)}, u32[]{:S(2)}, u32[]{:S(2)}) %collective-permute-start.4) | collective-permute-done | bytes 32800 | tf_op jit(solution)/shard_map/ppermute | solution.py:281
  77.7 0.4 collective-permute-start.5
  78.1 4.1 %collective-permute-done.5 = f32[64,128]{1,0:T(8,128)S(1)} collective-permute-done((f32[64,128]{1,0:T(8,128)S(1)}, f32[64,128]{1,0:T(8,128)S(1)}, u32[]{:S(2)}, u32[]{:S(2)}) %collective-permute-start.5) | collective-permute-done | bytes 32800 | tf_op jit(solution)/shard_map/ppermute | solution.py:281
  82.2 0.9 %collective-permute-start.6 = (f32[64,128]{1,0:T(8,128)S(1)}, f32[64,128]{1,0:T(8,128)S(1)}, u32[]{:S(2)}, u32[]{:S(2)}) collective-permute-start(f32[64,128]{1,0:T(8,128)S(1)} %add.26), channel_id=1, source_target_pairs={{0,97},{1,96},{2,99},{3,98},{4,101},{5,100},{6,103},{7,102},{8,105... | collective-permute-start | bytes 98312 | tf_op jit(solution)/shard_map/ppermute | solution.py:281
  83.1 3.6 %collective-permute-done.6 = f32[64,128]{1,0:T(8,128)S(1)} collective-permute-done((f32[64,128]{1,0:T(8,128)S(1)}, f32[64,128]{1,0:T(8,128)S(1)}, u32[]{:S(2)}, u32[]{:S(2)}) %collective-permute-start.6) | collective-permute-done | bytes 32800 | tf_op jit(solution)/shard_map/ppermute | solution.py:281
  86.8 0.6 broadcast_divide_fusion
  (11 shorter events, 0.1 us)
Async XLA Ops:
  0.1 48.7 %copy-start.1 = (bf16[1024,2048]{1,0:T(8,128)(2,1)S(1)}, bf16[1024,2048]{1,0:T(8,128)(2,1)}, u32[]{:S(2)}) copy-start(bf16[1024,2048]{1,0:T(8,128)(2,1)} %constant.19.clone.cos_ref) | copy-start | bytes 12582916
  4.3 44.4 %copy-start = (bf16[1024,2048]{1,0:T(8,128)(2,1)S(1)}, bf16[1024,2048]{1,0:T(8,128)(2,1)}, u32[]{:S(2)}) copy-start(bf16[1024,2048]{1,0:T(8,128)(2,1)} %constant.20.clone.sin_ref) | copy-start | bytes 12582916
  61.8 1.3 %collective-permute-start = (f32[64,128]{1,0:T(8,128)S(1)}, f32[64,128]{1,0:T(8,128)S(1)}, u32[]{:S(2)}, u32[]{:S(2)}) collective-permute-start(f32[64,128]{1,0:T(8,128)S(1)} %bins.1), channel_id=1, source_target_pairs={{0,1},{1,0},{2,3},{3,2},{4,5},{5,4},{6,7},{7,6},{8,9},{9,8},{10,11... | collective-permute-start | bytes 98312 | tf_op jit(solution)/shard_map/ppermute | solution.py:281
  63.1 3.3 %collective-permute-start.1 = (f32[64,128]{1,0:T(8,128)S(1)}, f32[64,128]{1,0:T(8,128)S(1)}, u32[]{:S(2)}, u32[]{:S(2)}) collective-permute-start(f32[64,128]{1,0:T(8,128)S(1)} %add.21), channel_id=1, source_target_pairs={{0,3},{1,2},{2,1},{3,0},{4,7},{5,6},{6,5},{7,4},{8,11},{9,10},{10,... | collective-permute-start | bytes 98312 | tf_op jit(solution)/shard_map/ppermute | solution.py:281
  66.4 3.3 %collective-permute-start.2 = (f32[64,128]{1,0:T(8,128)S(1)}, f32[64,128]{1,0:T(8,128)S(1)}, u32[]{:S(2)}, u32[]{:S(2)}) collective-permute-start(f32[64,128]{1,0:T(8,128)S(1)} %add.22), channel_id=1, source_target_pairs={{0,9},{1,8},{2,11},{3,10},{4,13},{5,12},{6,15},{7,14},{8,1},{9,0},... | collective-permute-start | bytes 98312 | tf_op jit(solution)/shard_map/ppermute | solution.py:281
  69.8 3.3 %collective-permute-start.3 = (f32[64,128]{1,0:T(8,128)S(1)}, f32[64,128]{1,0:T(8,128)S(1)}, u32[]{:S(2)}, u32[]{:S(2)}) collective-permute-start(f32[64,128]{1,0:T(8,128)S(1)} %add.23), channel_id=1, source_target_pairs={{0,33},{1,32},{2,35},{3,34},{4,37},{5,36},{6,39},{7,38},{8,41},{9,... | collective-permute-start | bytes 98312 | tf_op jit(solution)/shard_map/ppermute | solution.py:281
  73.1 4.6 %collective-permute-start.4 = (f32[64,128]{1,0:T(8,128)S(1)}, f32[64,128]{1,0:T(8,128)S(1)}, u32[]{:S(2)}, u32[]{:S(2)}) collective-permute-start(f32[64,128]{1,0:T(8,128)S(1)} %add.24), channel_id=1, source_target_pairs={{0,7},{1,6},{2,5},{3,4},{4,3},{5,2},{6,1},{7,0},{8,15},{9,14},{10,... | collective-permute-start | bytes 98312 | tf_op jit(solution)/shard_map/ppermute | solution.py:281
  77.7 4.6 %collective-permute-start.5 = (f32[64,128]{1,0:T(8,128)S(1)}, f32[64,128]{1,0:T(8,128)S(1)}, u32[]{:S(2)}, u32[]{:S(2)}) collective-permute-start(f32[64,128]{1,0:T(8,128)S(1)} %add.25), channel_id=1, source_target_pairs={{0,25},{1,24},{2,27},{3,26},{4,29},{5,28},{6,31},{7,30},{8,17},{9,... | collective-permute-start | bytes 98312 | tf_op jit(solution)/shard_map/ppermute | solution.py:281
  82.2 4.6 %collective-permute-start.6 = (f32[64,128]{1,0:T(8,128)S(1)}, f32[64,128]{1,0:T(8,128)S(1)}, u32[]{:S(2)}, u32[]{:S(2)}) collective-permute-start(f32[64,128]{1,0:T(8,128)S(1)} %add.26), channel_id=1, source_target_pairs={{0,97},{1,96},{2,99},{3,98},{4,101},{5,100},{6,103},{7,102},{8,105... | collective-permute-start | bytes 98312 | tf_op jit(solution)/shard_map/ppermute | solution.py:281
